TPU v7x, 512 devices: a whole 4x4x16 slice. The times are simulated.
512 devices in a mesh: inj: 4 (over y), blk: 128 (over z, x, core).
Axes of the slice: x: 4, y: 4, z: 16, core: 2. Of those that a mesh axis runs over, the one named last changes fastest.
Arguments:
- tile_values: bfloat16 [1536, 128, 128], P('blk'), may hold values from -0.3125 to 0.3125
- tile_row: int32 [1536], P('blk'), may hold values from 0 to 3
- tile_dest: int32 [1536, 1], P('blk'), may hold values from 0 to 6, as said below
- trans_block: int32 [128, 21], P('blk'), may hold values from 0 to 3
- inj_pores: int32 [256, 8192], P('inj', 'blk'), may hold values from 0 to 511
- final_weight: bfloat16 [256, 65536], P('inj', 'blk'), may hold values from -6 to 6
Outputs:
- sensitivity: bfloat16 [256, 65536], P('inj', 'blk')
- tile_gradient: bfloat16 [1536, 128, 128], P('blk', 'inj')
Inputs may be any that keep to these rules, and one draw needn't show every extreme that they name: `tile_dest`: among the tiles of one index of blk, every value is named by at most 3 tiles, and 0 by exactly 3 tiles.
All inputs are finite; a program needn't handle non-finite values.
Results may differ from a plain program's by a relative error of at most 0.014.
Values may be sent and summed in bfloat16 or wider, within the bound.
A program may use at most 64 MiB of HBM per device.

v0:
```python
import jax
import jax.numpy as jnp
from jax import lax
from jax.sharding import PartitionSpec as P

NEIGH = 6
STEPS = 4


def passed_along(block, axis, distance):
    devices = range(lax.axis_size(axis))
    route = [((i - distance) % len(devices), i) for i in devices]
    return lax.ppermute(block, axis, route)


def offset_of(slot):
    amount = (slot + 1) // 2
    return amount if slot % 2 == 1 else -amount


def shards(tile_values, tile_row, tile_dest, trans_block, inj_pores, final_weight):
    tile_count = tile_values.shape[0]
    block_width = tile_values.shape[1]
    set_count = final_weight.shape[0]
    pore_count = final_weight.shape[1]
    block_count = pore_count // block_width
    send_blocks = trans_block[0]
    slot_count = send_blocks.shape[0]
    neighbours = NEIGH
    capacity = slot_count // (neighbours + 1)
    targets = tile_dest[:, 0]
    ordinal = jnp.arange(tile_count, dtype=jnp.int32)
    earlier = ordinal[:, None] > ordinal[None, :]
    position = jnp.sum(((targets[:, None] == targets[None, :]) & earlier).astype(jnp.int32), axis=1)
    slot_index = targets * capacity + position
    block_ids = jnp.arange(block_count, dtype=jnp.int32)
    row_hot = (tile_row[:, None] == block_ids[None, :]).astype(jnp.float32)
    return_hot = (send_blocks[:, None] == block_ids[None, :]).astype(jnp.bfloat16)
    set_ids = jnp.arange(set_count, dtype=jnp.int32)[:, None]
    initial = jnp.zeros((set_count, pore_count), jnp.float32).at[set_ids, inj_pores].add(1.0)
    state = initial.astype(jnp.bfloat16).reshape(set_count, block_count, block_width)

    def piece_of(buffer, slot):
        return buffer[:, slot * capacity : (slot + 1) * capacity]

    adjoint = final_weight.reshape(set_count, block_count, block_width)
    fetched = [None] * STEPS
    saved_rows = [None] * STEPS
    for timestep in range(STEPS):
        fetch_outgoing = jnp.take(state, send_blocks, axis=1)
        fetch_pieces = [piece_of(fetch_outgoing, 0)]
        for fetch_slot in range(1, neighbours + 1):
            fetch_pieces.append(
                passed_along(piece_of(fetch_outgoing, fetch_slot), "blk", -offset_of(fetch_slot))
            )
        fetch_incoming = jnp.concatenate(fetch_pieces, axis=1)
        columns = jnp.take(fetch_incoming, slot_index, axis=1)
        fetched[timestep] = columns
        if timestep + 1 < STEPS:
            contrib = jnp.einsum(
                "sib,iab->sia", columns, tile_values, preferred_element_type=jnp.float32
            )
            state = jnp.einsum(
                "sia,ic->sca", contrib, row_hot, precision=lax.Precision.HIGHEST
            ).astype(jnp.bfloat16)
    for timestep in reversed(range(STEPS)):
        adjoint_rows = jnp.take(adjoint, tile_row, axis=1)
        saved_rows[timestep] = adjoint_rows
        outgoing = (
            jnp.zeros((set_count, slot_count, block_width), jnp.bfloat16)
            .at[:, slot_index, :]
            .set(
                jnp.einsum(
                    "sia,iab->sib", adjoint_rows, tile_values, preferred_element_type=jnp.float32
                ).astype(jnp.bfloat16)
            )
        )
        send_pieces = [piece_of(outgoing, 0)]
        for send_slot in range(1, neighbours + 1):
            send_pieces.append(
                passed_along(piece_of(outgoing, send_slot), "blk", offset_of(send_slot))
            )
        incoming = jnp.concatenate(send_pieces, axis=1)
        adjoint = jnp.einsum(
            "snb,nc->scb", incoming, return_hot, preferred_element_type=jnp.float32
        ).astype(jnp.bfloat16)
    accum = jnp.zeros((tile_count, block_width, block_width), jnp.float32)
    for timestep in range(STEPS):
        accum = accum + jnp.einsum(
            "sia,sib->iab",
            saved_rows[timestep],
            fetched[timestep],
            preferred_element_type=jnp.float32,
        )
    partial_sum = accum * (1.0 / set_count)
    summed = lax.psum(partial_sum.astype(jnp.bfloat16), "inj").astype(jnp.float32)
    portion = block_width // lax.axis_size("inj")
    mine = lax.dynamic_slice_in_dim(summed, lax.axis_index("inj") * portion, portion, 1)
    return (adjoint.reshape(set_count, pore_count), mine.astype(jnp.bfloat16))


def solution(mesh):
    placed = (
        P("blk", None, None),
        P("blk"),
        P("blk", None),
        P("blk", None),
        P("inj", "blk"),
        P("inj", "blk"),
    )
    return jax.shard_map(
        shards,
        mesh=mesh,
        in_specs=placed,
        out_specs=(P("inj", "blk"), P("blk", "inj", None)),
        check_vma=False,
    )
```

profile of v0, /device:TPU:1, one launch (start us, length us, event | category | flops | bytes accessed | tf_op | source)
XLA Modules:
  0.0 320.2 jit_solution(13132654927025406320)
XLA Ops:
  11.9 4.5 %collective-permute-start = (bf16[64,3,128]{2,1,0:T(4,128)(2,1)S(1)}, bf16[64,3,128]{2,1,0:T(4,128)(2,1)S(1)}, u32[]{:S(2)}, u32[]{:S(2)}) collective-permute-start(bf16[64,3,128]{2,1,0:T(4,128)(2,1)S(1)} %copy.158), channel_id=1, source_target_pairs={{127,0},{0,1},{1,2},{2,3},{3,4},{4,5},{5,6},{6,7},{7,8},{8,9},{9,1... | collective-permute-start | bytes 147464 | tf_op jit(solution)/shard_map/ppermute | solution.py:13
  16.4 6.2 %collective-permute-start.1 = (bf16[64,3,128]{2,1,0:T(4,128)(2,1)S(1)}, bf16[64,3,128]{2,1,0:T(4,128)(2,1)S(1)}, u32[]{:S(2)}, u32[]{:S(2)}) collective-permute-start(bf16[64,3,128]{2,1,0:T(4,128)(2,1)S(1)} %copy.159), channel_id=1, source_target_pairs={{1,0},{2,1},{3,2},{4,3},{5,4},{6,5},{7,6},{8,7},{9,8},{10,9},{11,1... | collective-permute-start | bytes 147464 | tf_op jit(solution)/shard_map/ppermute | solution.py:13
  24.7 7.9 %collective-permute-start.3 = (bf16[64,3,128]{2,1,0:T(4,128)(2,1)S(1)}, bf16[64,3,128]{2,1,0:T(4,128)(2,1)S(1)}, u32[]{:S(2)}, u32[]{:S(2)}) collective-permute-start(bf16[64,3,128]{2,1,0:T(4,128)(2,1)S(1)} %copy.161), channel_id=1, source_target_pairs={{2,0},{3,1},{4,2},{5,3},{6,4},{7,5},{8,6},{9,7},{10,8},{11,9},{12,... | collective-permute-start | bytes 147464 | tf_op jit(solution)/shard_map/ppermute | solution.py:13
  36.2 28.8 %scatter_custom_fusion.4 = f32[32768]{0:T(1024)S(1)} fusion(s32[4096]{0:T(1024)S(1)} %reshape.171, f32[4096]{0:T(1024)S(1)} %broadcast.101, f32[]{:T(128)} %constant.40.clone.1), kind=kCustom, calls=%fused_computation.80 | custom fusion | flops 4096 | bytes 131076
  65.9 7.0 %collective-permute-start.5 = (bf16[64,3,128]{2,1,0:T(4,128)(2,1)S(1)}, bf16[64,3,128]{2,1,0:T(4,128)(2,1)S(1)}, u32[]{:S(2)}, u32[]{:S(2)}) collective-permute-start(bf16[64,3,128]{2,1,0:T(4,128)(2,1)S(1)} %copy.163), channel_id=1, source_target_pairs={{3,0},{4,1},{5,2},{6,3},{7,4},{8,5},{9,6},{10,7},{11,8},{12,9},{13... | collective-permute-start | bytes 147464 | tf_op jit(solution)/shard_map/ppermute | solution.py:13
  72.9 7.3 %collective-permute-start.24 = (bf16[64,3,128]{2,0,1:T(8,128)(2,1)S(1)}, bf16[64,3,128]{2,0,1:T(8,128)(2,1)S(1)}, u32[]{:S(2)}, u32[]{:S(2)}) collective-permute-start(bf16[64,3,128]{2,0,1:T(8,128)(2,1)S(1)} %get-tuple-element.33), channel_id=1, source_target_pairs={{1,0},{2,1},{3,2},{4,3},{5,4},{6,5},{7,6},{8,7},{9,8},{10,9},{11,1... | collective-permute-start | bytes 147464 | tf_op jit(solution)/shard_map/ppermute | solution.py:13
  82.1 6.6 %collective-permute-start.26 = (bf16[64,3,128]{2,0,1:T(8,128)(2,1)S(1)}, bf16[64,3,128]{2,0,1:T(8,128)(2,1)S(1)}, u32[]{:S(2)}, u32[]{:S(2)}) collective-permute-start(bf16[64,3,128]{2,0,1:T(8,128)(2,1)S(1)} %get-tuple-element.31), channel_id=1, source_target_pairs={{2,0},{3,1},{4,2},{5,3},{6,4},{7,5},{8,6},{9,7},{10,8},{11,9},{12,... | collective-permute-start | bytes 147464 | tf_op jit(solution)/shard_map/ppermute | solution.py:13
  110.0 6.8 %collective-permute-start.9 = (bf16[64,3,128]{2,1,0:T(4,128)(2,1)S(1)}, bf16[64,3,128]{2,1,0:T(4,128)(2,1)S(1)}, u32[]{:S(2)}, u32[]{:S(2)}) collective-permute-start(bf16[64,3,128]{2,1,0:T(4,128)(2,1)S(1)} %copy.168), channel_id=1, source_target_pairs={{2,0},{3,1},{4,2},{5,3},{6,4},{7,5},{8,6},{9,7},{10,8},{11,9},{12,... | collective-permute-start | bytes 147464 | tf_op jit(solution)/shard_map/ppermute | solution.py:13
  121.2 7.0 %collective-permute-start.11 = (bf16[64,3,128]{2,1,0:T(4,128)(2,1)S(1)}, bf16[64,3,128]{2,1,0:T(4,128)(2,1)S(1)}, u32[]{:S(2)}, u32[]{:S(2)}) collective-permute-start(bf16[64,3,128]{2,1,0:T(4,128)(2,1)S(1)} %copy.170), channel_id=1, source_target_pairs={{3,0},{4,1},{5,2},{6,3},{7,4},{8,5},{9,6},{10,7},{11,8},{12,9},{13... | collective-permute-start | bytes 147464 | tf_op jit(solution)/shard_map/ppermute | solution.py:13
  128.3 7.4 %collective-permute-start.30 = (bf16[64,3,128]{2,0,1:T(8,128)(2,1)S(1)}, bf16[64,3,128]{2,0,1:T(8,128)(2,1)S(1)}, u32[]{:S(2)}, u32[]{:S(2)}) collective-permute-start(bf16[64,3,128]{2,0,1:T(8,128)(2,1)S(1)} %get-tuple-element.26), channel_id=1, source_target_pairs={{1,0},{2,1},{3,2},{4,3},{5,4},{6,5},{7,6},{8,7},{9,8},{10,9},{11,1... | collective-permute-start | bytes 147464 | tf_op jit(solution)/shard_map/ppermute | solution.py:13
  137.7 6.6 %collective-permute-start.32 = (bf16[64,3,128]{2,0,1:T(8,128)(2,1)S(1)}, bf16[64,3,128]{2,0,1:T(8,128)(2,1)S(1)}, u32[]{:S(2)}, u32[]{:S(2)}) collective-permute-start(bf16[64,3,128]{2,0,1:T(8,128)(2,1)S(1)} %get-tuple-element.24), channel_id=1, source_target_pairs={{2,0},{3,1},{4,2},{5,3},{6,4},{7,5},{8,6},{9,7},{10,8},{11,9},{12,... | collective-permute-start | bytes 147464 | tf_op jit(solution)/shard_map/ppermute | solution.py:13
  155.9 4.6 %collective-permute-done.35 = bf16[64,3,128]{2,0,1:T(8,128)(2,1)S(1)} collective-permute-done((bf16[64,3,128]{2,0,1:T(8,128)(2,1)S(1)}, bf16[64,3,128]{2,0,1:T(8,128)(2,1)S(1)}, u32[]{:S(2)}, u32[]{:S(2)}) %collective-permute-start.35) | collective-permute-done | bytes 49184 | tf_op jit(solution)/shard_map/ppermute | solution.py:13
  163.8 6.7 %collective-permute-start.12 = (bf16[64,3,128]{2,1,0:T(4,128)(2,1)S(1)}, bf16[64,3,128]{2,1,0:T(4,128)(2,1)S(1)}, u32[]{:S(2)}, u32[]{:S(2)}) collective-permute-start(bf16[64,3,128]{2,1,0:T(4,128)(2,1)S(1)} %copy.172), channel_id=1, source_target_pairs={{127,0},{0,1},{1,2},{2,3},{3,4},{4,5},{5,6},{6,7},{7,8},{8,9},{9,1... | collective-permute-start | bytes 147464 | tf_op jit(solution)/shard_map/ppermute | solution.py:13
  174.6 6.6 %collective-permute-start.15 = (bf16[64,3,128]{2,1,0:T(4,128)(2,1)S(1)}, bf16[64,3,128]{2,1,0:T(4,128)(2,1)}, u32[]{:S(2)}, u32[]{:S(2)}) collective-permute-start(bf16[64,3,128]{2,1,0:T(4,128)(2,1)S(1)} %copy.175), channel_id=1, source_target_pairs={{2,0},{3,1},{4,2},{5,3},{6,4},{7,5},{8,6},{9,7},{10,8},{11,9},{12,... | collective-permute-start | bytes 147464 | tf_op jit(solution)/shard_map/ppermute | solution.py:13
  184.6 7.0 %collective-permute-start.17 = (bf16[64,3,128]{2,1,0:T(4,128)(2,1)S(1)}, bf16[64,3,128]{2,1,0:T(4,128)(2,1)S(1)}, u32[]{:S(2)}, u32[]{:S(2)}) collective-permute-start(bf16[64,3,128]{2,1,0:T(4,128)(2,1)S(1)} %copy.177), channel_id=1, source_target_pairs={{3,0},{4,1},{5,2},{6,3},{7,4},{8,5},{9,6},{10,7},{11,8},{12,9},{13... | collective-permute-start | bytes 147464 | tf_op jit(solution)/shard_map/ppermute | solution.py:13
  197.6 6.6 %collective-permute-start.38 = (bf16[64,3,128]{2,0,1:T(8,128)(2,1)S(1)}, bf16[64,3,128]{2,0,1:T(8,128)(2,1)S(1)}, u32[]{:S(2)}, u32[]{:S(2)}) collective-permute-start(bf16[64,3,128]{2,0,1:T(8,128)(2,1)S(1)} %get-tuple-element.17), channel_id=1, source_target_pairs={{2,0},{3,1},{4,2},{5,3},{6,4},{7,5},{8,6},{9,7},{10,8},{11,9},{12,... | collective-permute-start | bytes 147464 | tf_op jit(solution)/shard_map/ppermute | solution.py:13
  212.7 4.5 %collective-permute-start.41 = (bf16[64,3,128]{2,0,1:T(8,128)(2,1)S(1)}, bf16[64,3,128]{2,0,1:T(8,128)(2,1)S(1)}, u32[]{:S(2)}, u32[]{:S(2)}) collective-permute-start(bf16[64,3,128]{2,0,1:T(8,128)(2,1)S(1)} %get-tuple-element.14), channel_id=1, source_target_pairs={{125,0},{126,1},{127,2},{0,3},{1,4},{2,5},{3,6},{4,7},{5,8},{6,9},... | collective-permute-start | bytes 147464 | tf_op jit(solution)/shard_map/ppermute | solution.py:13
  228.1 5.8 %collective-permute-start.43 = (bf16[64,3,128]{2,0,1:T(8,128)(2,1)S(1)}, bf16[64,3,128]{2,0,1:T(8,128)(2,1)S(1)}, u32[]{:S(2)}, u32[]{:S(2)}) collective-permute-start(bf16[64,3,128]{2,0,1:T(8,128)(2,1)S(1)} %get-tuple-element.11), channel_id=1, source_target_pairs={{127,0},{0,1},{1,2},{2,3},{3,4},{4,5},{5,6},{6,7},{7,8},{8,9},{9,1... | collective-permute-start | bytes 147464 | tf_op jit(solution)/shard_map/ppermute | solution.py:13
  233.9 5.5 %collective-permute-start.44 = (bf16[64,3,128]{2,0,1:T(8,128)(2,1)S(1)}, bf16[64,3,128]{2,0,1:T(8,128)(2,1)S(1)}, u32[]{:S(2)}, u32[]{:S(2)}) collective-permute-start(bf16[64,3,128]{2,0,1:T(8,128)(2,1)S(1)} %get-tuple-element.10), channel_id=1, source_target_pairs={{2,0},{3,1},{4,2},{5,3},{6,4},{7,5},{8,6},{9,7},{10,8},{11,9},{12,... | collective-permute-start | bytes 147464 | tf_op jit(solution)/shard_map/ppermute | solution.py:13
  245.2 4.5 %collective-permute-start.47 = (bf16[64,3,128]{2,0,1:T(8,128)(2,1)S(1)}, bf16[64,3,128]{2,0,1:T(8,128)(2,1)S(1)}, u32[]{:S(2)}, u32[]{:S(2)}) collective-permute-start(bf16[64,3,128]{2,0,1:T(8,128)(2,1)S(1)} %get-tuple-element.7), channel_id=1, source_target_pairs={{125,0},{126,1},{127,2},{0,3},{1,4},{2,5},{3,6},{4,7},{5,8},{6,9},... | collective-permute-start | bytes 147464 | tf_op jit(solution)/shard_map/ppermute | solution.py:13
  256.2 6.9 %collective-permute-start.18 = (bf16[64,3,128]{2,1,0:T(4,128)(2,1)S(1)}, bf16[64,3,128]{2,1,0:T(4,128)(2,1)S(1)}, u32[]{:S(2)}, u32[]{:S(2)}) collective-permute-start(bf16[64,3,128]{2,1,0:T(4,128)(2,1)S(1)} %copy.179), channel_id=1, source_target_pairs={{127,0},{0,1},{1,2},{2,3},{3,4},{4,5},{5,6},{6,7},{7,8},{8,9},{9,1... | collective-permute-start | bytes 147464 | tf_op jit(solution)/shard_map/ppermute | solution.py:13
  267.1 6.6 %collective-permute-start.21 = (bf16[64,3,128]{2,1,0:T(4,128)(2,1)S(1)}, bf16[64,3,128]{2,1,0:T(4,128)(2,1)S(1)}, u32[]{:S(2)}, u32[]{:S(2)}) collective-permute-start(bf16[64,3,128]{2,1,0:T(4,128)(2,1)S(1)} %copy.182), channel_id=1, source_target_pairs={{2,0},{3,1},{4,2},{5,3},{6,4},{7,5},{8,6},{9,7},{10,8},{11,9},{12,... | collective-permute-start | bytes 147464 | tf_op jit(solution)/shard_map/ppermute | solution.py:13
  275.8 7.0 %collective-permute-start.23 = (bf16[64,3,128]{2,1,0:T(4,128)(2,1)S(1)}, bf16[64,3,128]{2,1,0:T(4,128)(2,1)S(1)}, u32[]{:S(2)}, u32[]{:S(2)}) collective-permute-start(bf16[64,3,128]{2,1,0:T(4,128)(2,1)S(1)} %copy.184), channel_id=1, source_target_pairs={{3,0},{4,1},{5,2},{6,3},{7,4},{8,5},{9,6},{10,7},{11,8},{12,9},{13... | collective-permute-start | bytes 147464 | tf_op jit(solution)/shard_map/ppermute | solution.py:13
  286.2 25.6 %all-reduce.2.cloned.1.call-done = bf16[12,128,128]{2,1,0:T(8,128)(2,1)} async-done(((bf16[12,128,128]{2,1,0:T(8,128)(2,1)}), bf16[12,128,128]{2,1,0:T(8,128)(2,1)}) %all-reduce.2.cloned.1.call-update) | async-done | bytes 393232 | tf_op jit(solution)/shard_map/psum | solution.py:96
  (240 shorter events, 110.8 us)
Async XLA Ops:
  7.2 304.6 %all-reduce.2.cloned.1.call-start = ((), (), s32[]{:S(2)}) async-start(), calls=%async_computation | async-start | bytes 786432 | tf_op jit(solution)/shard_map/psum | solution.py:96
  11.9 54.0 %collective-permute-start = (bf16[64,3,128]{2,1,0:T(4,128)(2,1)S(1)}, bf16[64,3,128]{2,1,0:T(4,128)(2,1)S(1)}, u32[]{:S(2)}, u32[]{:S(2)}) collective-permute-start(bf16[64,3,128]{2,1,0:T(4,128)(2,1)S(1)} %copy.158), channel_id=1, source_target_pairs={{127,0},{0,1},{1,2},{2,3},{3,4},{4,5},{5,6},{6,7},{7,8},{8,9},{9,1... | collective-permute-start | bytes 147464 | tf_op jit(solution)/shard_map/ppermute | solution.py:13
  16.4 56.5 %collective-permute-start.1 = (bf16[64,3,128]{2,1,0:T(4,128)(2,1)S(1)}, bf16[64,3,128]{2,1,0:T(4,128)(2,1)S(1)}, u32[]{:S(2)}, u32[]{:S(2)}) collective-permute-start(bf16[64,3,128]{2,1,0:T(4,128)(2,1)S(1)} %copy.159), channel_id=1, source_target_pairs={{1,0},{2,1},{3,2},{4,3},{5,4},{6,5},{7,6},{8,7},{9,8},{10,9},{11,1... | collective-permute-start | bytes 147464 | tf_op jit(solution)/shard_map/ppermute | solution.py:13
  22.7 57.5 %collective-permute-start.2 = (bf16[64,3,128]{2,1,0:T(4,128)(2,1)S(1)}, bf16[64,3,128]{2,1,0:T(4,128)(2,1)S(1)}, u32[]{:S(2)}, u32[]{:S(2)}) collective-permute-start(bf16[64,3,128]{2,1,0:T(4,128)(2,1)S(1)} %copy.160), channel_id=1, source_target_pairs={{126,0},{127,1},{0,2},{1,3},{2,4},{3,5},{4,6},{5,7},{6,8},{7,9},{8... | collective-permute-start | bytes 147464 | tf_op jit(solution)/shard_map/ppermute | solution.py:13
  24.7 57.4 %collective-permute-start.3 = (bf16[64,3,128]{2,1,0:T(4,128)(2,1)S(1)}, bf16[64,3,128]{2,1,0:T(4,128)(2,1)S(1)}, u32[]{:S(2)}, u32[]{:S(2)}) collective-permute-start(bf16[64,3,128]{2,1,0:T(4,128)(2,1)S(1)} %copy.161), channel_id=1, source_target_pairs={{2,0},{3,1},{4,2},{5,3},{6,4},{7,5},{8,6},{9,7},{10,8},{11,9},{12,... | collective-permute-start | bytes 147464 | tf_op jit(solution)/shard_map/ppermute | solution.py:13
  32.7 56.0 %collective-permute-start.4 = (bf16[64,3,128]{2,1,0:T(4,128)(2,1)S(1)}, bf16[64,3,128]{2,1,0:T(4,128)(2,1)S(1)}, u32[]{:S(2)}, u32[]{:S(2)}) collective-permute-start(bf16[64,3,128]{2,1,0:T(4,128)(2,1)S(1)} %copy.162), channel_id=1, source_target_pairs={{125,0},{126,1},{127,2},{0,3},{1,4},{2,5},{3,6},{4,7},{5,8},{6,9},... | collective-permute-start | bytes 147464 | tf_op jit(solution)/shard_map/ppermute | solution.py:13
  65.9 24.8 %collective-permute-start.5 = (bf16[64,3,128]{2,1,0:T(4,128)(2,1)S(1)}, bf16[64,3,128]{2,1,0:T(4,128)(2,1)S(1)}, u32[]{:S(2)}, u32[]{:S(2)}) collective-permute-start(bf16[64,3,128]{2,1,0:T(4,128)(2,1)S(1)} %copy.163), channel_id=1, source_target_pairs={{3,0},{4,1},{5,2},{6,3},{7,4},{8,5},{9,6},{10,7},{11,8},{12,9},{13... | collective-permute-start | bytes 147464 | tf_op jit(solution)/shard_map/ppermute | solution.py:13
  72.9 24.2 %collective-permute-start.24 = (bf16[64,3,128]{2,0,1:T(8,128)(2,1)S(1)}, bf16[64,3,128]{2,0,1:T(8,128)(2,1)S(1)}, u32[]{:S(2)}, u32[]{:S(2)}) collective-permute-start(bf16[64,3,128]{2,0,1:T(8,128)(2,1)S(1)} %get-tuple-element.33), channel_id=1, source_target_pairs={{1,0},{2,1},{3,2},{4,3},{5,4},{6,5},{7,6},{8,7},{9,8},{10,9},{11,1... | collective-permute-start | bytes 147464 | tf_op jit(solution)/shard_map/ppermute | solution.py:13
  80.2 21.3 %collective-permute-start.25 = (bf16[64,3,128]{2,0,1:T(8,128)(2,1)S(1)}, bf16[64,3,128]{2,0,1:T(8,128)(2,1)S(1)}, u32[]{:S(2)}, u32[]{:S(2)}) collective-permute-start(bf16[64,3,128]{2,0,1:T(8,128)(2,1)S(1)} %get-tuple-element.32), channel_id=1, source_target_pairs={{127,0},{0,1},{1,2},{2,3},{3,4},{4,5},{5,6},{6,7},{7,8},{8,9},{9,1... | collective-permute-start | bytes 147464 | tf_op jit(solution)/shard_map/ppermute | solution.py:13
  82.1 23.8 %collective-permute-start.26 = (bf16[64,3,128]{2,0,1:T(8,128)(2,1)S(1)}, bf16[64,3,128]{2,0,1:T(8,128)(2,1)S(1)}, u32[]{:S(2)}, u32[]{:S(2)}) collective-permute-start(bf16[64,3,128]{2,0,1:T(8,128)(2,1)S(1)} %get-tuple-element.31), channel_id=1, source_target_pairs={{2,0},{3,1},{4,2},{5,3},{6,4},{7,5},{8,6},{9,7},{10,8},{11,9},{12,... | collective-permute-start | bytes 147464 | tf_op jit(solution)/shard_map/ppermute | solution.py:13
  105.9 22.4 %collective-permute-start.7 = (bf16[64,3,128]{2,1,0:T(4,128)(2,1)S(1)}, bf16[64,3,128]{2,1,0:T(4,128)(2,1)S(1)}, u32[]{:S(2)}, u32[]{:S(2)}) collective-permute-start(bf16[64,3,128]{2,1,0:T(4,128)(2,1)S(1)} %copy.166), channel_id=1, source_target_pairs={{1,0},{2,1},{3,2},{4,3},{5,4},{6,5},{7,6},{8,7},{9,8},{10,9},{11,1... | collective-permute-start | bytes 147464 | tf_op jit(solution)/shard_map/ppermute | solution.py:13
  107.9 27.8 %collective-permute-start.8 = (bf16[64,3,128]{2,1,0:T(4,128)(2,1)S(1)}, bf16[64,3,128]{2,1,0:T(4,128)(2,1)S(1)}, u32[]{:S(2)}, u32[]{:S(2)}) collective-permute-start(bf16[64,3,128]{2,1,0:T(4,128)(2,1)S(1)} %copy.167), channel_id=1, source_target_pairs={{126,0},{127,1},{0,2},{1,3},{2,4},{3,5},{4,6},{5,7},{6,8},{7,9},{8... | collective-permute-start | bytes 147464 | tf_op jit(solution)/shard_map/ppermute | solution.py:13
  110.0 27.6 %collective-permute-start.9 = (bf16[64,3,128]{2,1,0:T(4,128)(2,1)S(1)}, bf16[64,3,128]{2,1,0:T(4,128)(2,1)S(1)}, u32[]{:S(2)}, u32[]{:S(2)}) collective-permute-start(bf16[64,3,128]{2,1,0:T(4,128)(2,1)S(1)} %copy.168), channel_id=1, source_target_pairs={{2,0},{3,1},{4,2},{5,3},{6,4},{7,5},{8,6},{9,7},{10,8},{11,9},{12,... | collective-permute-start | bytes 147464 | tf_op jit(solution)/shard_map/ppermute | solution.py:13
  116.9 27.4 %collective-permute-start.10 = (bf16[64,3,128]{2,1,0:T(4,128)(2,1)S(1)}, bf16[64,3,128]{2,1,0:T(4,128)(2,1)S(1)}, u32[]{:S(2)}, u32[]{:S(2)}) collective-permute-start(bf16[64,3,128]{2,1,0:T(4,128)(2,1)S(1)} %copy.169), channel_id=1, source_target_pairs={{125,0},{126,1},{127,2},{0,3},{1,4},{2,5},{3,6},{4,7},{5,8},{6,9},... | collective-permute-start | bytes 147464 | tf_op jit(solution)/shard_map/ppermute | solution.py:13
  121.2 25.0 %collective-permute-start.11 = (bf16[64,3,128]{2,1,0:T(4,128)(2,1)S(1)}, bf16[64,3,128]{2,1,0:T(4,128)(2,1)S(1)}, u32[]{:S(2)}, u32[]{:S(2)}) collective-permute-start(bf16[64,3,128]{2,1,0:T(4,128)(2,1)S(1)} %copy.170), channel_id=1, source_target_pairs={{3,0},{4,1},{5,2},{6,3},{7,4},{8,5},{9,6},{10,7},{11,8},{12,9},{13... | collective-permute-start | bytes 147464 | tf_op jit(solution)/shard_map/ppermute | solution.py:13
  128.3 23.1 %collective-permute-start.30 = (bf16[64,3,128]{2,0,1:T(8,128)(2,1)S(1)}, bf16[64,3,128]{2,0,1:T(8,128)(2,1)S(1)}, u32[]{:S(2)}, u32[]{:S(2)}) collective-permute-start(bf16[64,3,128]{2,0,1:T(8,128)(2,1)S(1)} %get-tuple-element.26), channel_id=1, source_target_pairs={{1,0},{2,1},{3,2},{4,3},{5,4},{6,5},{7,6},{8,7},{9,8},{10,9},{11,1... | collective-permute-start | bytes 147464 | tf_op jit(solution)/shard_map/ppermute | solution.py:13
  170.5 21.2 %collective-permute-start.13 = (bf16[64,3,128]{2,1,0:T(4,128)(2,1)S(1)}, bf16[64,3,128]{2,1,0:T(4,128)(2,1)S(1)}, u32[]{:S(2)}, u32[]{:S(2)}) collective-permute-start(bf16[64,3,128]{2,1,0:T(4,128)(2,1)S(1)} %copy.173), channel_id=1, source_target_pairs={{1,0},{2,1},{3,2},{4,3},{5,4},{6,5},{7,6},{8,7},{9,8},{10,9},{11,1... | collective-permute-start | bytes 147464 | tf_op jit(solution)/shard_map/ppermute | solution.py:13
  172.5 23.2 %collective-permute-start.14 = (bf16[64,3,128]{2,1,0:T(4,128)(2,1)S(1)}, bf16[64,3,128]{2,1,0:T(4,128)(2,1)}, u32[]{:S(2)}, u32[]{:S(2)}) collective-permute-start(bf16[64,3,128]{2,1,0:T(4,128)(2,1)S(1)} %copy.174), channel_id=1, source_target_pairs={{126,0},{127,1},{0,2},{1,3},{2,4},{3,5},{4,6},{5,7},{6,8},{7,9},{8... | collective-permute-start | bytes 147464 | tf_op jit(solution)/shard_map/ppermute | solution.py:13
  174.6 23.0 %collective-permute-start.15 = (bf16[64,3,128]{2,1,0:T(4,128)(2,1)S(1)}, bf16[64,3,128]{2,1,0:T(4,128)(2,1)}, u32[]{:S(2)}, u32[]{:S(2)}) collective-permute-start(bf16[64,3,128]{2,1,0:T(4,128)(2,1)S(1)} %copy.175), channel_id=1, source_target_pairs={{2,0},{3,1},{4,2},{5,3},{6,4},{7,5},{8,6},{9,7},{10,8},{11,9},{12,... | collective-permute-start | bytes 147464 | tf_op jit(solution)/shard_map/ppermute | solution.py:13
  181.2 23.0 %collective-permute-start.16 = (bf16[64,3,128]{2,1,0:T(4,128)(2,1)S(1)}, bf16[64,3,128]{2,1,0:T(4,128)(2,1)}, u32[]{:S(2)}, u32[]{:S(2)}) collective-permute-start(bf16[64,3,128]{2,1,0:T(4,128)(2,1)S(1)} %copy.176), channel_id=1, source_target_pairs={{125,0},{126,1},{127,2},{0,3},{1,4},{2,5},{3,6},{4,7},{5,8},{6,9},... | collective-permute-start | bytes 147464 | tf_op jit(solution)/shard_map/ppermute | solution.py:13
  184.6 21.5 %collective-permute-start.17 = (bf16[64,3,128]{2,1,0:T(4,128)(2,1)S(1)}, bf16[64,3,128]{2,1,0:T(4,128)(2,1)S(1)}, u32[]{:S(2)}, u32[]{:S(2)}) collective-permute-start(bf16[64,3,128]{2,1,0:T(4,128)(2,1)S(1)} %copy.177), channel_id=1, source_target_pairs={{3,0},{4,1},{5,2},{6,3},{7,4},{8,5},{9,6},{10,7},{11,8},{12,9},{13... | collective-permute-start | bytes 147464 | tf_op jit(solution)/shard_map/ppermute | solution.py:13
  191.7 21.0 %collective-permute-start.36 = (bf16[64,3,128]{2,0,1:T(8,128)(2,1)S(1)}, bf16[64,3,128]{2,0,1:T(8,128)(2,1)S(1)}, u32[]{:S(2)}, u32[]{:S(2)}) collective-permute-start(bf16[64,3,128]{2,0,1:T(8,128)(2,1)S(1)} %get-tuple-element.19), channel_id=1, source_target_pairs={{1,0},{2,1},{3,2},{4,3},{5,4},{6,5},{7,6},{8,7},{9,8},{10,9},{11,1... | collective-permute-start | bytes 147464 | tf_op jit(solution)/shard_map/ppermute | solution.py:13
  195.7 21.6 %collective-permute-start.37 = (bf16[64,3,128]{2,0,1:T(8,128)(2,1)S(1)}, bf16[64,3,128]{2,0,1:T(8,128)(2,1)S(1)}, u32[]{:S(2)}, u32[]{:S(2)}) collective-permute-start(bf16[64,3,128]{2,0,1:T(8,128)(2,1)S(1)} %get-tuple-element.18), channel_id=1, source_target_pairs={{127,0},{0,1},{1,2},{2,3},{3,4},{4,5},{5,6},{6,7},{7,8},{8,9},{9,1... | collective-permute-start | bytes 147464 | tf_op jit(solution)/shard_map/ppermute | solution.py:13
  228.1 21.6 %collective-permute-start.43 = (bf16[64,3,128]{2,0,1:T(8,128)(2,1)S(1)}, bf16[64,3,128]{2,0,1:T(8,128)(2,1)S(1)}, u32[]{:S(2)}, u32[]{:S(2)}) collective-permute-start(bf16[64,3,128]{2,0,1:T(8,128)(2,1)S(1)} %get-tuple-element.11), channel_id=1, source_target_pairs={{127,0},{0,1},{1,2},{2,3},{3,4},{4,5},{5,6},{6,7},{7,8},{8,9},{9,1... | collective-permute-start | bytes 147464 | tf_op jit(solution)/shard_map/ppermute | solution.py:13
  (40 other events, 625.7 us)
Sparse Core Ops, SparseCore 0:
  256.2 55.5 all-reduce.1
where the time goes:
time: 323 us; the launch traced here: 320 us
  starting transfers between devices  200 us (62%)
  waiting for transfers between devices  39.7 us (12%)
  other arithmetic  31.8 us (10%)
  local copies, waits for them, and re-layouts  25.6 us (8%)
  between operations  15.7 us (5%)
  matrix products  7.15 us (2%)
    ppermute x48, starting transfers between devices, passed_along(): return lax.ppermute(block, axis, route)  200 us
    unnamed x4, other arithmetic  28.9 us
    psum x1, waiting for transfers between devices, shards(): lax.psum(partial_sum.astype(jnp.bfloat16), 'inj').astype(jnp.float32)  25.6 us
    ppermute x48, waiting for transfers between devices, passed_along(): return lax.ppermute(block, axis, route)  14.1 us
    concatenate x4, local copies, waits for them, and re-layouts, shards(): incoming = jnp.concatenate(send_pieces, axis=1)  7.51 us
  transfers between devices with their start and end apart: 49, of which 6 were waited for; matrix products, arithmetic and copies ran while one was open for 15% of the time, Pallas kernels for 0%

commit v1 on v0

v1 whole, which is shorter than its diff:
```python
import functools

import jax
import jax.numpy as jnp
from jax import lax
from jax.experimental import pallas as pl
from jax.experimental.pallas import tpu as pltpu
from jax.sharding import PartitionSpec as P

NEIGH = 6
STEPS = 4
CAP = 3
SLOTS = (NEIGH + 1) * CAP
HALVES = 2
MESH = pl.DeviceIdType.MESH
F32 = jnp.float32
BF16 = jnp.bfloat16


def offset_of(slot):
    amount = (slot + 1) // 2
    return amount if slot % 2 == 1 else -amount


def dot_nt(x, y):
    return lax.dot_general(x, y, (((1,), (1,)), ((), ())), preferred_element_type=F32)


def dot_nn(x, y):
    return lax.dot_general(x, y, (((1,), (0,)), ((), ())), preferred_element_type=F32)


def sweep(
    n_inj, n_blk, blocks, tiles_dev, row_in, dest_in, trans_in, tiles_hbm, pores_hbm, weight_hbm,
    sens_ref, grad_ref, tiles, pores, state, adj, adj_t, terms, fsend, bsend, brecv, gsend, grecv,
    slot_s, tile_s, rowmask, transmask, in_sem, fs_sem, fr_sem, bs_sem, br_sem, gs_sem, gr_sem, *fetched,
):
    me_i, me_b = lax.axis_index("inj"), lax.axis_index("blk")
    sets = pores.shape[0]
    hs = sets // HALVES
    width = tiles.shape[-1]
    portion = width // n_inj

    def at_blk(distance):
        return (me_i, lax.rem(me_b + (distance + n_blk), n_blk))

    def at_inj(distance):
        return lax.rem(me_i + distance, n_inj)

    barrier = pltpu.get_barrier_semaphore()
    for j in range(1, NEIGH + 1):
        pl.semaphore_signal(barrier, inc=1, device_id=at_blk(offset_of(j)), device_id_type=MESH)
    for o in range(1, n_inj):
        pl.semaphore_signal(barrier, inc=1, device_id=(at_inj(o), me_b), device_id_type=MESH)

    loads = [
        pltpu.make_async_copy(pores_hbm, pores, in_sem.at[0]),
        pltpu.make_async_copy(tiles_hbm, tiles, in_sem.at[1]),
    ]
    for c in range(blocks):
        loads.append(
            pltpu.make_async_copy(
                weight_hbm.at[:, pl.ds(c * width, width)],
                adj.at[c, pl.ds((STEPS - 1) * sets, sets)],
                in_sem.at[2 + c],
            )
        )
    for load in loads:
        load.start()

    dests = [dest_in[i, 0] for i in range(tiles_dev)]
    slots = []
    for i in range(tiles_dev):
        earlier = jnp.int32(0)
        for e in range(i):
            earlier = earlier + jnp.where(dests[e] == dests[i], 1, 0)
        slots.append(dests[i] * CAP + earlier)
        slot_s[i] = slots[i]
    for n in range(SLOTS):
        user = jnp.int32(tiles_dev)
        for i in range(tiles_dev):
            user = jnp.where(slots[i] == n, i, user)
        tile_s[n] = user
    for i in range(tiles_dev):
        for r in range(blocks):
            rowmask[i * blocks + r] = jnp.where(row_in[i] == r, 1.0, 0.0).astype(F32)
    for n in range(SLOTS):
        for c in range(blocks):
            transmask[n * blocks + c] = jnp.where(trans_in[0, n] == c, 1.0, 0.0).astype(F32)
    terms[tiles_dev] = jnp.zeros_like(terms[tiles_dev])

    def f_copy(t, h, j):
        span = pl.ds(j * CAP, CAP)
        return pltpu.make_async_remote_copy(
            fsend.at[t, h, span], fetched[t * HALVES + h].at[span],
            fs_sem.at[t, h, j - 1], fr_sem.at[t, h, j - 1],
            device_id=at_blk(-offset_of(j)), device_id_type=MESH,
        )

    def b_copy(t, h, j):
        span = pl.ds(j * CAP, CAP)
        return pltpu.make_async_remote_copy(
            bsend.at[t, h, span], brecv.at[t, h, span],
            bs_sem.at[t, h, j - 1], br_sem.at[t, h, j - 1],
            device_id=at_blk(offset_of(j)), device_id_type=MESH,
        )

    def f_fill(t, h):
        for n in range(SLOTS):
            block = state[trans_in[0, n], pl.ds(h * hs, hs)]
            if n < CAP:
                fetched[t * HALVES + h][n] = block
            else:
                fsend[t, h, n] = block

    def b_fill(t, h):
        where = pl.ds(t * sets + h * hs, hs)
        for i in range(tiles_dev):
            terms[i] = dot_nn(adj[row_in[i], where], tiles[i]).astype(BF16)
        for n in range(SLOTS):
            block = terms[tile_s[n]]
            if n < CAP:
                brecv[t, h, n] = block
            else:
                bsend[t, h, n] = block

    def f_step(t, h):
        total = [None] * blocks
        for i in range(tiles_dev):
            part = dot_nt(fetched[t * HALVES + h][slot_s[i]], tiles[i])
            for r in range(blocks):
                kept = part * rowmask[i * blocks + r]
                total[r] = kept if total[r] is None else total[r] + kept
        for r in range(blocks):
            state[r, pl.ds(h * hs, hs)] = total[r].astype(BF16)

    def b_step(t, h):
        total = [None] * blocks
        for n in range(SLOTS):
            part = brecv[t, h, n].astype(F32)
            for c in range(blocks):
                kept = part * transmask[n * blocks + c]
                total[c] = kept if total[c] is None else total[c] + kept
        return total

    loads[0].wait()
    ids = pores[...]
    low = lax.bitwise_and(ids, width - 1)
    unit = lax.shift_left(jnp.ones_like(ids), lax.shift_right_logical(ids, 7) * 8)
    lanes = lax.broadcasted_iota(jnp.int32, (sets, width), 1)
    counts = jnp.zeros((sets, width), jnp.int32)
    for e in range(ids.shape[1]):
        counts = counts + jnp.where(low[:, e : e + 1] == lanes, unit[:, e : e + 1], 0)
    for c in range(blocks):
        one = lax.bitwise_and(lax.shift_right_logical(counts, 8 * c), 255)
        state[c] = one.astype(F32).astype(BF16)
    for h in range(HALVES):
        f_fill(0, h)
    pl.semaphore_wait(barrier, NEIGH + n_inj - 1)
    for h in range(HALVES):
        for j in range(1, NEIGH + 1):
            f_copy(0, h, j).start()
    for load in loads[1:]:
        load.wait()
    for h in range(HALVES):
        b_fill(STEPS - 1, h)
        for j in range(1, NEIGH + 1):
            b_copy(STEPS - 1, h, j).start()

    def transpose_pair(p):
        for r in range(blocks):
            both = adj[r, pl.ds(p * 2 * sets, 2 * sets)]
            adj_t[r, :, pl.ds(p * 2 * sets, 2 * sets)] = both.T

    for k in range(STEPS):
        last = k == STEPS - 1
        for h in range(HALVES):
            for j in range(1, NEIGH + 1):
                f_copy(k, h, j).wait_recv()
            if not last:
                f_step(k, h)
                f_fill(k + 1, h)
                for j in range(1, NEIGH + 1):
                    f_copy(k + 1, h, j).start()
        if last:
            for i in range(tiles_dev):
                columns = jnp.concatenate(
                    [fetched[t * HALVES + h][slot_s[i]] for t in range(STEPS) for h in range(HALVES)], axis=0
                )
                full = dot_nn(adj_t[row_in[i]], columns) * (1.0 / sets)
                full = full.astype(BF16)
                for p in range(n_inj):
                    gsend[p, i] = full[p * portion : (p + 1) * portion]
            g_copies = []
            for o in range(1, n_inj):
                to = at_inj(o)
                g_copies.append(
                    pltpu.make_async_remote_copy(
                        gsend.at[to], grecv.at[o - 1], gs_sem.at[o - 1], gr_sem.at[o - 1],
                        device_id=(to, me_b), device_id_type=MESH,
                    )
                )
                g_copies[-1].start()
        back = STEPS - 1 - k
        for h in range(HALVES):
            for j in range(1, NEIGH + 1):
                b_copy(back, h, j).wait_recv()
            total = b_step(back, h)
            if last:
                for c in range(blocks):
                    sens_ref[pl.ds(h * hs, hs), pl.ds(c * width, width)] = total[c].astype(BF16)
            else:
                for c in range(blocks):
                    adj[c, pl.ds((back - 1) * sets + h * hs, hs)] = total[c].astype(BF16)
                b_fill(back - 1, h)
                for j in range(1, NEIGH + 1):
                    b_copy(back - 1, h, j).start()
        if k == 0:
            transpose_pair(1)
        if k == STEPS - 2:
            transpose_pair(0)
    for copy in g_copies:
        copy.wait_recv()
    mine = gsend[me_i].astype(F32)
    for o in range(1, n_inj):
        mine = mine + grecv[o - 1].astype(F32)
    grad_ref[...] = mine.astype(BF16)
    for copy in g_copies:
        copy.wait_send()
    for t in range(STEPS):
        for h in range(HALVES):
            for j in range(1, NEIGH + 1):
                f_copy(t, h, j).wait_send()
                b_copy(t, h, j).wait_send()


def shards(tile_values, tile_row, tile_dest, trans_block, inj_pores, final_weight):
    tiles_dev, width = tile_values.shape[:2]
    sets, pores = final_weight.shape
    blocks = pores // width
    n_inj, n_blk = lax.axis_size("inj"), lax.axis_size("blk")
    portion = width // n_inj
    hs = sets // HALVES
    smem = pl.BlockSpec(memory_space=pltpu.SMEM)
    hbm = pl.BlockSpec(memory_space=pl.ANY)
    vmem = pl.BlockSpec(memory_space=pltpu.VMEM)
    dma = pltpu.SemaphoreType.DMA
    return pl.pallas_call(
        functools.partial(sweep, n_inj, n_blk, blocks, tiles_dev),
        name="sweep",
        out_shape=(
            jax.ShapeDtypeStruct((sets, pores), BF16),
            jax.ShapeDtypeStruct((tiles_dev, portion, width), BF16),
        ),
        in_specs=[smem, smem, smem, hbm, hbm, hbm],
        out_specs=(vmem, vmem),
        scratch_shapes=[
            pltpu.VMEM((tiles_dev, width, width), BF16),
            pltpu.VMEM(inj_pores.shape, jnp.int32),
            pltpu.VMEM((blocks, sets, width), BF16),
            pltpu.VMEM((blocks, STEPS * sets, width), BF16),
            pltpu.VMEM((blocks, width, STEPS * sets), BF16),
            pltpu.VMEM((tiles_dev + 1, hs, width), BF16),
            pltpu.VMEM((STEPS, HALVES, SLOTS, hs, width), BF16),
            pltpu.VMEM((STEPS, HALVES, SLOTS, hs, width), BF16),
            pltpu.VMEM((STEPS, HALVES, SLOTS, hs, width), BF16),
            pltpu.VMEM((n_inj, tiles_dev, portion, width), BF16),
            pltpu.VMEM((n_inj - 1, tiles_dev, portion, width), BF16),
            pltpu.SMEM((tiles_dev,), jnp.int32),
            pltpu.SMEM((SLOTS,), jnp.int32),
            pltpu.SMEM((tiles_dev * blocks,), F32),
            pltpu.SMEM((SLOTS * blocks,), F32),
            dma((2 + blocks,)),
            dma((STEPS, HALVES, NEIGH)),
            dma((STEPS, HALVES, NEIGH)),
            dma((STEPS, HALVES, NEIGH)),
            dma((STEPS, HALVES, NEIGH)),
            dma((n_inj - 1,)),
            dma((n_inj - 1,)),
        ]
        + [pltpu.VMEM((SLOTS, hs, width), BF16)] * (STEPS * HALVES),
        compiler_params=pltpu.CompilerParams(
            collective_id=0, has_side_effects=True, vmem_limit_bytes=32 * 1024 * 1024
        ),
    )(tile_row, tile_dest, trans_block, tile_values, inj_pores, final_weight)


def solution(mesh):
    placed = (
        P("blk", None, None),
        P("blk"),
        P("blk", None),
        P("blk", None),
        P("inj", "blk"),
        P("inj", "blk"),
    )
    return jax.shard_map(
        shards,
        mesh=mesh,
        in_specs=placed,
        out_specs=(P("inj", "blk"), P("blk", "inj", None)),
        check_vma=False,
    )
```

time: 323 us -> 56.3 us (0.17)
  starting transfers between devices: 200 us -> 0 us
  Pallas kernels: 0 us -> 50.7 us
  waiting for transfers between devices: 39.7 us -> 0 us
  other arithmetic: 31.8 us -> 0 us
  local copies, waits for them, and re-layouts: 25.6 us -> 4.63 us
  between operations: 15.7 us -> 0.66 us
  matrix products: 7.15 us -> 0 us
    ppermute x48 -> x0, starting transfers between devices: 200 us -> none  [passed_along(): return lax.ppermute(block, axis, route)]
    pallas_call x0 -> x1, Pallas kernels: none -> 50.7 us  [shards(): pl.pallas_call(functools.partial(sweep, n_inj, n_blk, blocks, tiles_dev),...]
    unnamed x4 -> x0, other arithmetic: 28.9 us -> none
    psum x1 -> x0, waiting for transfers between devices: 25.6 us -> none  [shards(): lax.psum(partial_sum.astype(jnp.bfloat16), 'inj').astype(jnp.float32)]
    ppermute x48 -> x0, waiting for transfers between devices: 14.1 us -> none  [passed_along(): return lax.ppermute(block, axis, route)]
    concatenate x8 -> x0, local copies, waits for them, and re-layouts: 7.56 us -> none  [the longest x4 7.51 us: shards(): incoming = jnp.concatenate(send_pieces, axis=1)]
    gather x12 -> x0, local copies, waits for them, and re-layouts: 7.37 us -> none  [the longest x4 2.7 us: shards(): fetch_outgoing = jnp.take(state, send_blocks, axis=1)]
    dot_general x18 -> x0, matrix products: 7.15 us -> none  [the longest x4 2.43 us: shards(): jnp.einsum('sia,sib->iab', saved_rows[timestep], fetched[timestep], prefe...]
  transfers between devices with their start and end apart: 49 -> 0, of which waited for: 6 -> 0; matrix products, arithmetic and copies ran while one was open for 15% -> 0% of each run, Pallas kernels for 0% -> 0%
where the time goes in v1:
time: 56.3 us; the launch traced here: 56 us
  Pallas kernels  50.7 us (90%)
  local copies, waits for them, and re-layouts  4.63 us (8%)
  between operations  0.66 us (1%)
    pallas_call x1, Pallas kernels, shards(): pl.pallas_call(functools.partial(sweep, n_inj, n_blk, blocks, tiles_dev),...  50.7 us
    unnamed x13, local copies, waits for them, and re-layouts  4.63 us

profile of v1, /device:TPU:1, one launch (start us, length us, event | category | flops | bytes accessed | tf_op | source)
XLA Modules:
  0.0 56.0 jit_solution(11779795706354954809)
XLA Ops:
  0.6 0.0 copy-start.4
  0.6 0.0 copy-start.3
  0.7 0.8 %copy.8.dest_in = s32[12,1]{1,0:T(8,128)S(1)} copy(s32[12,1]{0,1:T(1,128)} %param.8) | data formatting | bytes 96 | tf_op args[2]
  1.4 0.0 copy-done.4
  1.4 0.0 copy-done.3
  1.4 0.0 copy-start
  1.4 1.0 %copy-done = bf16[12,128,128]{2,1,0:T(8,128)(2,1)S(1)} copy-done((bf16[12,128,128]{2,1,0:T(8,128)(2,1)S(1)}, bf16[12,128,128]{2,1,0:T(8,128)(2,1)}, u32[]{:S(2)}) %copy-start) | copy-done | bytes 393240
  2.4 0.0 copy-start.1
  2.4 0.8 %copy-done.1 = bf16[64,512]{1,0:T(8,128)(2,1)S(1)} copy-done((bf16[64,512]{1,0:T(8,128)(2,1)S(1)}, bf16[64,512]{1,0:T(8,128)(2,1)}, u32[]{:S(2)}) %copy-start.1) | copy-done | bytes 65560
  3.2 0.0 copy-start.2
  3.3 0.8 %copy-done.2 = s32[64,64]{1,0:T(8,128)S(1)} copy-done((s32[64,64]{1,0:T(8,128)S(1)}, s32[64,64]{1,0:T(8,128)}, u32[]{:S(2)}) %copy-start.2) | copy-done | bytes 16408
  4.0 50.7 %sweep.1 = (bf16[64,512]{1,0:T(8,128)(2,1)S(1)}, bf16[12,32,128]{2,1,0:T(8,128)(2,1)S(1)}) custom-call(s32[12]{0:T(128)S(1)} %copy-done.3, s32[12,1]{1,0:T(8,128)S(1)} %copy.8.dest_in, s32[1,21]{1,0:T(1,128)S(1)} %copy-done.4, bf16[12,128,128]{2,1,0:T(8,128)(2,1)S(1)} %copy-done, s32[64,64]{1,0:T(8,128)S(1)} %copy-done.2, bf16[64,512]{1,0:T(8,128)(2,1)S(1)} %copy-done.1), custom_call_target="tpu_custom_call" | custom-call | tf_op jit(solution)/shard_map/sweep/pallas_call | solution.py:248
  54.8 0.6 %copy.11 = bf16[64,512]{1,0:T(8,128)(2,1)} copy(bf16[64,512]{1,0:T(8,128)(2,1)S(1)} %get-tuple-element.4) | data formatting | bytes 131072
  55.4 0.6 %copy.12 = bf16[12,32,128]{2,1,0:T(8,128)(2,1)} copy(bf16[12,32,128]{2,1,0:T(8,128)(2,1)S(1)} %get-tuple-element.5) | data formatting | bytes 196608
Async XLA Ops:
  0.6 0.8 %copy-start.4 = (s32[1,21]{1,0:T(1,128)S(1)}, s32[1,21]{1,0:T(1,128)}, u32[]{:S(2)}) copy-start(s32[1,21]{1,0:T(1,128)} %trans_in.1) | copy-start | bytes 256
  0.6 0.8 %copy-start.3 = (s32[12]{0:T(128)S(1)}, s32[12]{0:T(128)}, u32[]{:S(2)}) copy-start(s32[12]{0:T(128)} %row_in.1) | copy-start | bytes 148
  1.4 1.0 %copy-start = (bf16[12,128,128]{2,1,0:T(8,128)(2,1)S(1)}, bf16[12,128,128]{2,1,0:T(8,128)(2,1)}, u32[]{:S(2)}) copy-start(bf16[12,128,128]{2,1,0:T(8,128)(2,1)} %tiles_hbm.1) | copy-start | bytes 1179652
  2.4 0.8 %copy-start.1 = (bf16[64,512]{1,0:T(8,128)(2,1)S(1)}, bf16[64,512]{1,0:T(8,128)(2,1)}, u32[]{:S(2)}) copy-start(bf16[64,512]{1,0:T(8,128)(2,1)} %weight_hbm.1) | copy-start | bytes 196612
  3.2 0.8 %copy-start.2 = (s32[64,64]{1,0:T(8,128)S(1)}, s32[64,64]{1,0:T(8,128)}, u32[]{:S(2)}) copy-start(s32[64,64]{1,0:T(8,128)} %pores_hbm.1) | copy-start | bytes 49156

commit v2 on v1

v2 whole, which is shorter than its diff:
```python
import functools

import jax
import jax.numpy as jnp
from jax import lax
from jax.experimental import pallas as pl
from jax.experimental.pallas import tpu as pltpu
from jax.sharding import PartitionSpec as P

NEIGH = 6
STEPS = 4
CAP = 3
SLOTS = (NEIGH + 1) * CAP
HF = 1
HB = 1
MESH = pl.DeviceIdType.MESH
F32 = jnp.float32
BF16 = jnp.bfloat16


def offset_of(slot):
    amount = (slot + 1) // 2
    return amount if slot % 2 == 1 else -amount


def dot_nt(x, y):
    return lax.dot_general(x, y, (((1,), (1,)), ((), ())), preferred_element_type=F32)


def dot_nn(x, y):
    return lax.dot_general(x, y, (((1,), (0,)), ((), ())), preferred_element_type=F32)


def sweep(
    n_inj, n_blk, blocks, tiles_dev, row_hbm, dest_hbm, trans_hbm, tiles_hbm, pores_hbm, weight_hbm,
    sens_hbm, parts_hbm, row_in, dest_in, trans_in, sens_ref, tiles, pores, state, adj, adj_t, terms, fsend, bsend, brecv, gsend,
    slot_s, tile_s, rowmask, transmask, in_sem, fs_sem, fr_sem, bs_sem, br_sem, gs_sem, gr_sem, *fetched,
):
    me_i, me_b = lax.axis_index("inj"), lax.axis_index("blk")
    sets = pores.shape[0]
    fs, bs = sets // HF, sets // HB
    width = tiles.shape[-1]
    portion = width // n_inj

    def at_blk(distance):
        return (me_i, lax.rem(me_b + (distance + n_blk), n_blk))

    def at_inj(distance):
        return lax.rem(me_i + distance, n_inj)

    small = [
        pltpu.make_async_copy(trans_hbm, trans_in, in_sem.at[4 + blocks]),
        pltpu.make_async_copy(row_hbm, row_in, in_sem.at[5 + blocks]),
        pltpu.make_async_copy(dest_hbm, dest_in, in_sem.at[6 + blocks]),
    ]
    loads = [
        pltpu.make_async_copy(pores_hbm, pores, in_sem.at[0]),
        pltpu.make_async_copy(tiles_hbm, tiles, in_sem.at[1]),
    ]
    for c in range(blocks):
        loads.append(
            pltpu.make_async_copy(
                weight_hbm.at[:, pl.ds(c * width, width)],
                adj.at[c, pl.ds((STEPS - 1) * sets, sets)],
                in_sem.at[2 + c],
            )
        )
    loads[0].start()
    for load in small + loads[1:]:
        load.start()

    barrier = pltpu.get_barrier_semaphore()
    for j in range(1, NEIGH + 1):
        pl.semaphore_signal(barrier, inc=1, device_id=at_blk(offset_of(j)), device_id_type=MESH)
    for o in range(1, n_inj):
        pl.semaphore_signal(barrier, inc=1, device_id=(at_inj(o), me_b), device_id_type=MESH)

    def f_copy(t, h, j):
        span = pl.ds(j * CAP, CAP)
        return pltpu.make_async_remote_copy(
            fsend.at[t, h, span], fetched[t * HF + h].at[span],
            fs_sem.at[t, h, j - 1], fr_sem.at[t, h, j - 1],
            device_id=at_blk(-offset_of(j)), device_id_type=MESH,
        )

    def b_copy(t, h, j):
        span = pl.ds(j * CAP, CAP)
        return pltpu.make_async_remote_copy(
            bsend.at[t, h, span], brecv.at[t, h, span],
            bs_sem.at[t, h, j - 1], br_sem.at[t, h, j - 1],
            device_id=at_blk(offset_of(j)), device_id_type=MESH,
        )

    def f_start(t, h):
        for j in range(1, NEIGH + 1):
            f_copy(t, h, j).start()

    def b_start(t, h):
        for j in range(1, NEIGH + 1):
            b_copy(t, h, j).start()

    def f_fill(t, h):
        for n in range(SLOTS):
            block = state[trans_in[0, n], pl.ds(h * fs, fs)]
            if n < CAP:
                fetched[t * HF + h][n] = block
            else:
                fsend[t, h, n] = block

    def b_fill(t, h):
        where = pl.ds(t * sets + h * bs, bs)
        for i in range(tiles_dev):
            terms[i] = dot_nn(adj[row_in[i], where], tiles[i]).astype(BF16)
        for n in range(SLOTS):
            block = terms[tile_s[n]]
            if n < CAP:
                brecv[t, h, n] = block
            else:
                bsend[t, h, n] = block

    def f_step(t, h):
        total = [None] * blocks
        for i in range(tiles_dev):
            part = dot_nt(fetched[t * HF + h][slot_s[i]], tiles[i])
            for r in range(blocks):
                kept = part * rowmask[i * blocks + r]
                total[r] = kept if total[r] is None else total[r] + kept
        for r in range(blocks):
            state[r, pl.ds(h * fs, fs)] = total[r].astype(BF16)

    def b_step(t, h):
        total = [None] * blocks
        for n in range(SLOTS):
            part = brecv[t, h, n].astype(F32)
            for c in range(blocks):
                kept = part * transmask[n * blocks + c]
                total[c] = kept if total[c] is None else total[c] + kept
        return total

    loads[0].wait()
    ids = pores[...]
    low = lax.bitwise_and(ids, width - 1)
    unit = lax.shift_left(jnp.ones_like(ids), lax.shift_right_logical(ids, 7) * 8)
    lanes = lax.broadcasted_iota(jnp.int32, (sets, width), 1)
    counts = jnp.zeros((sets, width), jnp.int32)
    for e in range(ids.shape[1]):
        counts = counts + jnp.where(low[:, e : e + 1] == lanes, unit[:, e : e + 1], 0)
    for c in range(blocks):
        one = lax.bitwise_and(lax.shift_right_logical(counts, 8 * c), 255)
        state[c] = one.astype(F32).astype(BF16)
    small[0].wait()
    for h in range(HF):
        f_fill(0, h)
    pl.semaphore_wait(barrier, NEIGH + n_inj - 1)
    for h in range(HF):
        f_start(0, h)
    small[1].wait()
    small[2].wait()

    dests = [dest_in[i] for i in range(tiles_dev)]
    slots = []
    for i in range(tiles_dev):
        earlier = jnp.int32(0)
        for e in range(i):
            earlier = earlier + jnp.where(dests[e] == dests[i], 1, 0)
        slots.append(dests[i] * CAP + earlier)
        slot_s[i] = slots[i]
    for n in range(SLOTS):
        user = jnp.int32(tiles_dev)
        for i in range(tiles_dev):
            user = jnp.where(slots[i] == n, i, user)
        tile_s[n] = user
    for i in range(tiles_dev):
        for r in range(blocks):
            rowmask[i * blocks + r] = jnp.where(row_in[i] == r, 1.0, 0.0).astype(F32)
    for n in range(SLOTS):
        for c in range(blocks):
            transmask[n * blocks + c] = jnp.where(trans_in[0, n] == c, 1.0, 0.0).astype(F32)
    terms[tiles_dev] = jnp.zeros_like(terms[tiles_dev])

    for load in loads[1:]:
        load.wait()
    for h in range(HB):
        b_fill(STEPS - 1, h)
    for h in range(HB):
        b_start(STEPS - 1, h)

    def transpose_pair(p):
        for r in range(blocks):
            both = adj[r, pl.ds(p * 2 * sets, 2 * sets)]
            adj_t[r, :, pl.ds(p * 2 * sets, 2 * sets)] = both.T

    for k in range(STEPS):
        last = k == STEPS - 1
        back = STEPS - 1 - k
        for h in range(HF):
            for j in range(1, NEIGH + 1):
                f_copy(k, h, j).wait_recv()
            if not last:
                f_step(k, h)
                f_fill(k + 1, h)
                f_start(k + 1, h)
        if last:
            for h in range(HB):
                b_start(0, h)
            for i in range(tiles_dev):
                columns = jnp.concatenate(
                    [fetched[t * HF + h][slot_s[i]] for t in range(STEPS) for h in range(HF)], axis=0
                )
                full = dot_nn(adj_t[row_in[i]], columns) * (1.0 / sets)
                full = full.astype(BF16)
                for p in range(n_inj):
                    gsend[p, i] = full[p * portion : (p + 1) * portion]
            own_out = pltpu.make_async_copy(gsend.at[me_i], parts_hbm.at[0], in_sem.at[3 + blocks])
            g_copies = []
            for o in range(1, n_inj):
                to = at_inj(o)
                g_copies.append(
                    pltpu.make_async_remote_copy(
                        gsend.at[to], parts_hbm.at[o], gs_sem.at[o - 1], gr_sem.at[o - 1],
                        device_id=(to, me_b), device_id_type=MESH,
                    )
                )
                g_copies[-1].start()
            own_out.start()
        for h in range(HB):
            for j in range(1, NEIGH + 1):
                b_copy(back, h, j).wait_recv()
            total = b_step(back, h)
            for c in range(blocks):
                if last:
                    sens_ref[pl.ds(h * bs, bs), pl.ds(c * width, width)] = total[c].astype(BF16)
                else:
                    adj[c, pl.ds((back - 1) * sets + h * bs, bs)] = total[c].astype(BF16)
            if not last:
                b_fill(back - 1, h)
                if back > 1:
                    b_start(back - 1, h)
        if k == 0:
            transpose_pair(1)
        if k == STEPS - 2:
            transpose_pair(0)
    sens_out = pltpu.make_async_copy(sens_ref, sens_hbm, in_sem.at[2 + blocks])
    sens_out.start()
    for copy in g_copies:
        copy.wait_recv()
    for copy in g_copies:
        copy.wait_send()
    for t in range(STEPS):
        for j in range(1, NEIGH + 1):
            for h in range(HF):
                f_copy(t, h, j).wait_send()
            for h in range(HB):
                b_copy(t, h, j).wait_send()
    sens_out.wait()
    own_out.wait()


def shards(tile_values, tile_row, tile_dest, trans_block, inj_pores, final_weight):
    tiles_dev, width = tile_values.shape[:2]
    sets, pores = final_weight.shape
    blocks = pores // width
    n_inj, n_blk = lax.axis_size("inj"), lax.axis_size("blk")
    portion = width // n_inj
    fs, bs = sets // HF, sets // HB
    hbm = pl.BlockSpec(memory_space=pl.ANY)
    dma = pltpu.SemaphoreType.DMA
    sensitivity, parts = pl.pallas_call(
        functools.partial(sweep, n_inj, n_blk, blocks, tiles_dev),
        name="sweep",
        out_shape=(
            jax.ShapeDtypeStruct((sets, pores), BF16),
            jax.ShapeDtypeStruct((n_inj, tiles_dev, portion, width), BF16),
        ),
        in_specs=[hbm] * 6,
        out_specs=(hbm, hbm),
        scratch_shapes=[
            pltpu.SMEM((tiles_dev,), jnp.int32),
            pltpu.SMEM((tiles_dev,), jnp.int32),
            pltpu.SMEM(trans_block.shape, jnp.int32),
            pltpu.VMEM((sets, pores), BF16),
            pltpu.VMEM((tiles_dev, width, width), BF16),
            pltpu.VMEM(inj_pores.shape, jnp.int32),
            pltpu.VMEM((blocks, sets, width), BF16),
            pltpu.VMEM((blocks, STEPS * sets, width), BF16),
            pltpu.VMEM((blocks, width, STEPS * sets), BF16),
            pltpu.VMEM((tiles_dev + 1, bs, width), BF16),
            pltpu.VMEM((STEPS, HF, SLOTS, fs, width), BF16),
            pltpu.VMEM((STEPS, HB, SLOTS, bs, width), BF16),
            pltpu.VMEM((STEPS, HB, SLOTS, bs, width), BF16),
            pltpu.VMEM((n_inj, tiles_dev, portion, width), BF16),
            pltpu.SMEM((tiles_dev,), jnp.int32),
            pltpu.SMEM((SLOTS,), jnp.int32),
            pltpu.SMEM((tiles_dev * blocks,), F32),
            pltpu.SMEM((SLOTS * blocks,), F32),
            dma((7 + blocks,)),
            dma((STEPS, HF, NEIGH)),
            dma((STEPS, HF, NEIGH)),
            dma((STEPS, HB, NEIGH)),
            dma((STEPS, HB, NEIGH)),
            dma((n_inj - 1,)),
            dma((n_inj - 1,)),
        ]
        + [pltpu.VMEM((SLOTS, fs, width), BF16)] * (STEPS * HF),
        compiler_params=pltpu.CompilerParams(
            collective_id=0, has_side_effects=True, vmem_limit_bytes=60 * 1024 * 1024
        ),
    )(tile_row, tile_dest[:, 0], trans_block, tile_values, inj_pores, final_weight)
    total = parts[0].astype(F32)
    for o in range(1, n_inj):
        total = total + parts[o].astype(F32)
    return sensitivity, total.astype(BF16)


def solution(mesh):
    placed = (
        P("blk", None, None),
        P("blk"),
        P("blk", None),
        P("blk", None),
        P("inj", "blk"),
        P("inj", "blk"),
    )
    return jax.shard_map(
        shards,
        mesh=mesh,
        in_specs=placed,
        out_specs=(P("inj", "blk"), P("blk", "inj", None)),
        check_vma=False,
    )
```

time: 56.3 us -> 52.4 us (0.931)
  local copies, waits for them, and re-layouts: 4.63 us -> 0.63 us
  other arithmetic: 0 us -> 1.76 us
  Pallas kernels: 50.7 us -> 49.2 us
    unnamed x13 -> x3, local copies, waits for them, and re-layouts: 4.63 us -> 0.63 us
    add x0 -> x1, other arithmetic: none -> 1.76 us  [shards(): total = total + parts[o].astype(F32)]
    pallas_call x1, Pallas kernels: 50.7 us -> 49.2 us  [shards(): pl.pallas_call(functools.partial(sweep, n_inj, n_blk, blocks, tiles_dev),...]
where the time goes in v2:
time: 52.4 us; the launch traced here: 52.2 us
  Pallas kernels  49.2 us (94%)
  other arithmetic  1.76 us (3%)
  between operations  0.65 us (1%)
  local copies, waits for them, and re-layouts  0.63 us (1%)
    pallas_call x1, Pallas kernels, shards(): pl.pallas_call(functools.partial(sweep, n_inj, n_blk, blocks, tiles_dev),...  49.2 us
    add x1, other arithmetic, shards(): total = total + parts[o].astype(F32)  1.76 us

profile of v2, /device:TPU:1, one launch (start us, length us, event | category | flops | bytes accessed | tf_op | source)
XLA Modules:
  0.0 52.2 jit_solution(8978504490204682720)
XLA Ops:
  0.6 49.2 %sweep.1 = (bf16[64,512]{1,0:T(8,128)(2,1)}, bf16[4,12,32,128]{3,2,1,0:T(8,128)(2,1)}) custom-call(s32[12]{0:T(128)} %row_hbm.1, s32[12]{0:T(128)} %bitcast.3, s32[1,21]{1,0:T(1,128)} %trans_hbm.1, bf16[12,128,128]{2,1,0:T(8,128)(2,1)} %tiles_hbm.1, s32[64,64]{1,0:T(8,128)} %pores_hbm.1, bf16[64,512]{1,0:T(8,128)(2,1)} %weight_hbm.1), custom_call_target="tpu_custom_call" | custom-call | tf_op jit(solution)/shard_map/sweep/pallas_call | solution.py:268
  49.8 0.0 copy-start
  49.8 1.8 %fusion = bf16[12,32,128]{2,1,0:T(8,128)(2,1)} fusion(bf16[4,12,32,128]{3,2,1,0:T(8,128)(2,1)} %get-tuple-element.5), kind=kLoop, calls=%fused_computation.1 | loop fusion | flops 393216 | bytes 491520 | tf_op jit(solution)/shard_map/add | solution.py:311
  51.6 0.0 copy-done
  51.6 0.6 %copy.9 = bf16[64,512]{1,0:T(8,128)(2,1)} copy(bf16[64,512]{1,0:T(8,128)(2,1)S(1)} %copy-done) | data formatting | bytes 131072
Async XLA Ops:
  49.8 1.8 %copy-start = (bf16[64,512]{1,0:T(8,128)(2,1)S(1)}, bf16[64,512]{1,0:T(8,128)(2,1)}, u32[]{:S(2)}) copy-start(bf16[64,512]{1,0:T(8,128)(2,1)} %get-tuple-element.8) | copy-start | bytes 196612

commit v3 on v2

--- a/solution.py
+++ b/solution.py
@@ -11,8 +11,8 @@
 STEPS = 4
 CAP = 3
 SLOTS = (NEIGH + 1) * CAP
-HF = 1
-HB = 1
+HF = 2
+HB = 2
 MESH = pl.DeviceIdType.MESH
 F32 = jnp.float32
 BF16 = jnp.bfloat16
@@ -33,7 +33,7 @@
 
 def sweep(
     n_inj, n_blk, blocks, tiles_dev, row_hbm, dest_hbm, trans_hbm, tiles_hbm, pores_hbm, weight_hbm,
-    sens_hbm, parts_hbm, row_in, dest_in, trans_in, sens_ref, tiles, pores, state, adj, adj_t, terms, fsend, bsend, brecv, gsend,
+    sens_ref, grad_ref, row_in, dest_in, trans_in, tiles, pores, state, adj, adj_t, terms, fsend, bsend, brecv, gsend, grecv,
     slot_s, tile_s, rowmask, transmask, in_sem, fs_sem, fr_sem, bs_sem, br_sem, gs_sem, gr_sem, *fetched,
 ):
     me_i, me_b = lax.axis_index("inj"), lax.axis_index("blk")
@@ -49,9 +49,9 @@
         return lax.rem(me_i + distance, n_inj)
 
     small = [
-        pltpu.make_async_copy(trans_hbm, trans_in, in_sem.at[4 + blocks]),
-        pltpu.make_async_copy(row_hbm, row_in, in_sem.at[5 + blocks]),
-        pltpu.make_async_copy(dest_hbm, dest_in, in_sem.at[6 + blocks]),
+        pltpu.make_async_copy(trans_hbm, trans_in, in_sem.at[2 + blocks]),
+        pltpu.make_async_copy(row_hbm, row_in, in_sem.at[3 + blocks]),
+        pltpu.make_async_copy(dest_hbm, dest_in, in_sem.at[4 + blocks]),
     ]
     loads = [
         pltpu.make_async_copy(pores_hbm, pores, in_sem.at[0]),
@@ -75,19 +75,19 @@
     for o in range(1, n_inj):
         pl.semaphore_signal(barrier, inc=1, device_id=(at_inj(o), me_b), device_id_type=MESH)
 
-    def f_copy(t, h, j):
-        span = pl.ds(j * CAP, CAP)
+    def f_copy(t, h, j, count=1):
+        span = pl.ds(j * CAP, count * CAP)
         return pltpu.make_async_remote_copy(
             fsend.at[t, h, span], fetched[t * HF + h].at[span],
-            fs_sem.at[t, h, j - 1], fr_sem.at[t, h, j - 1],
+            fs_sem.at[t, h], fr_sem.at[t, h],
             device_id=at_blk(-offset_of(j)), device_id_type=MESH,
         )
 
-    def b_copy(t, h, j):
-        span = pl.ds(j * CAP, CAP)
+    def b_copy(t, h, j, count=1):
+        span = pl.ds(j * CAP, count * CAP)
         return pltpu.make_async_remote_copy(
             bsend.at[t, h, span], brecv.at[t, h, span],
-            bs_sem.at[t, h, j - 1], br_sem.at[t, h, j - 1],
+            bs_sem.at[t, h], br_sem.at[t, h],
             device_id=at_blk(offset_of(j)), device_id_type=MESH,
         )
 
@@ -95,9 +95,15 @@
         for j in range(1, NEIGH + 1):
             f_copy(t, h, j).start()
 
+    def f_all(t, h):
+        return f_copy(t, h, 1, NEIGH)
+
     def b_start(t, h):
         for j in range(1, NEIGH + 1):
             b_copy(t, h, j).start()
+
+    def b_all(t, h):
+        return b_copy(t, h, 1, NEIGH)
 
     def f_fill(t, h):
         for n in range(SLOTS):
@@ -194,8 +200,9 @@
         last = k == STEPS - 1
         back = STEPS - 1 - k
         for h in range(HF):
-            for j in range(1, NEIGH + 1):
-                f_copy(k, h, j).wait_recv()
+            if k:
+                f_all(k - 1, h).wait_send()
+            f_all(k, h).wait_recv()
             if not last:
                 f_step(k, h)
                 f_fill(k + 1, h)
@@ -211,21 +218,20 @@
                 full = full.astype(BF16)
                 for p in range(n_inj):
                     gsend[p, i] = full[p * portion : (p + 1) * portion]
-            own_out = pltpu.make_async_copy(gsend.at[me_i], parts_hbm.at[0], in_sem.at[3 + blocks])
             g_copies = []
             for o in range(1, n_inj):
                 to = at_inj(o)
                 g_copies.append(
                     pltpu.make_async_remote_copy(
-                        gsend.at[to], parts_hbm.at[o], gs_sem.at[o - 1], gr_sem.at[o - 1],
+                        gsend.at[to], grecv.at[o - 1], gs_sem.at[o - 1], gr_sem.at[o - 1],
                         device_id=(to, me_b), device_id_type=MESH,
                     )
                 )
                 g_copies[-1].start()
-            own_out.start()
         for h in range(HB):
-            for j in range(1, NEIGH + 1):
-                b_copy(back, h, j).wait_recv()
+            if k:
+                b_all(back + 1, h).wait_send()
+            b_all(back, h).wait_recv()
             total = b_step(back, h)
             for c in range(blocks):
                 if last:
@@ -240,20 +246,18 @@
             transpose_pair(1)
         if k == STEPS - 2:
             transpose_pair(0)
-    sens_out = pltpu.make_async_copy(sens_ref, sens_hbm, in_sem.at[2 + blocks])
-    sens_out.start()
+    for h in range(HF):
+        f_all(STEPS - 1, h).wait_send()
+    for h in range(HB):
+        b_all(0, h).wait_send()
     for copy in g_copies:
         copy.wait_recv()
+    mine = gsend[me_i].astype(F32)
+    for o in range(1, n_inj):
+        mine = mine + grecv[o - 1].astype(F32)
+    grad_ref[...] = mine.astype(BF16)
     for copy in g_copies:
         copy.wait_send()
-    for t in range(STEPS):
-        for j in range(1, NEIGH + 1):
-            for h in range(HF):
-                f_copy(t, h, j).wait_send()
-            for h in range(HB):
-                b_copy(t, h, j).wait_send()
-    sens_out.wait()
-    own_out.wait()
 
 
 def shards(tile_values, tile_row, tile_dest, trans_block, inj_pores, final_weight):
@@ -263,22 +267,19 @@
     n_inj, n_blk = lax.axis_size("inj"), lax.axis_size("blk")
     portion = width // n_inj
     fs, bs = sets // HF, sets // HB
+    vmem = pl.BlockSpec(memory_space=pltpu.VMEM)
     hbm = pl.BlockSpec(memory_space=pl.ANY)
     dma = pltpu.SemaphoreType.DMA
-    sensitivity, parts = pl.pallas_call(
+    return pl.pallas_call(
         functools.partial(sweep, n_inj, n_blk, blocks, tiles_dev),
         name="sweep",
-        out_shape=(
-            jax.ShapeDtypeStruct((sets, pores), BF16),
-            jax.ShapeDtypeStruct((n_inj, tiles_dev, portion, width), BF16),
-        ),
+        out_shape=(pltpu.VMEM((sets, pores), BF16), pltpu.VMEM((tiles_dev, portion, width), BF16)),
         in_specs=[hbm] * 6,
-        out_specs=(hbm, hbm),
+        out_specs=(vmem, vmem),
         scratch_shapes=[
             pltpu.SMEM((tiles_dev,), jnp.int32),
             pltpu.SMEM((tiles_dev,), jnp.int32),
             pltpu.SMEM(trans_block.shape, jnp.int32),
-            pltpu.VMEM((sets, pores), BF16),
             pltpu.VMEM((tiles_dev, width, width), BF16),
             pltpu.VMEM(inj_pores.shape, jnp.int32),
             pltpu.VMEM((blocks, sets, width), BF16),
@@ -289,15 +290,16 @@
             pltpu.VMEM((STEPS, HB, SLOTS, bs, width), BF16),
             pltpu.VMEM((STEPS, HB, SLOTS, bs, width), BF16),
             pltpu.VMEM((n_inj, tiles_dev, portion, width), BF16),
+            pltpu.VMEM((n_inj - 1, tiles_dev, portion, width), BF16),
             pltpu.SMEM((tiles_dev,), jnp.int32),
             pltpu.SMEM((SLOTS,), jnp.int32),
             pltpu.SMEM((tiles_dev * blocks,), F32),
             pltpu.SMEM((SLOTS * blocks,), F32),
-            dma((7 + blocks,)),
-            dma((STEPS, HF, NEIGH)),
-            dma((STEPS, HF, NEIGH)),
-            dma((STEPS, HB, NEIGH)),
-            dma((STEPS, HB, NEIGH)),
+            dma((5 + blocks,)),
+            dma((STEPS, HF)),
+            dma((STEPS, HF)),
+            dma((STEPS, HB)),
+            dma((STEPS, HB)),
             dma((n_inj - 1,)),
             dma((n_inj - 1,)),
         ]
@@ -306,10 +308,6 @@
             collective_id=0, has_side_effects=True, vmem_limit_bytes=60 * 1024 * 1024
         ),
     )(tile_row, tile_dest[:, 0], trans_block, tile_values, inj_pores, final_weight)
-    total = parts[0].astype(F32)
-    for o in range(1, n_inj):
-        total = total + parts[o].astype(F32)
-    return sensitivity, total.astype(BF16)
 
 
 def solution(mesh):

time: 52.4 us -> 49.5 us (0.945)
  other arithmetic: 1.76 us -> 0 us
  Pallas kernels: 49.2 us -> 47.5 us
  local copies, waits for them, and re-layouts: 0.63 us -> 1.27 us
    add x1 -> x0, other arithmetic: 1.76 us -> none  [shards(): total = total + parts[o].astype(F32)]
    pallas_call x1, Pallas kernels: 49.2 us -> 47.5 us  [shards(): pl.pallas_call(functools.partial(sweep, n_inj, n_blk, blocks, tiles_dev),...]
    unnamed x3 -> x2, local copies, waits for them, and re-layouts: 0.63 us -> 1.27 us
where the time goes in v3:
time: 49.5 us; the launch traced here: 49.4 us
  Pallas kernels  47.5 us (96%)
  local copies, waits for them, and re-layouts  1.27 us (3%)
  between operations  0.64 us (1%)
    pallas_call x1, Pallas kernels, shards(): pl.pallas_call(functools.partial(sweep, n_inj, n_blk, blocks, tiles_dev),...  47.5 us
    unnamed x2, local copies, waits for them, and re-layouts  1.27 us

profile of v3, /device:TPU:1, one launch (start us, length us, event | category | flops | bytes accessed | tf_op | source)
XLA Modules:
  0.0 49.4 jit_solution(15089966856202693652)
XLA Ops:
  0.6 47.5 %sweep.1 = (bf16[64,512]{1,0:T(8,128)(2,1)S(1)}, bf16[12,32,128]{2,1,0:T(8,128)(2,1)S(1)}) custom-call(s32[12]{0:T(128)} %row_hbm.1, s32[12]{0:T(128)} %bitcast.1, s32[1,21]{1,0:T(1,128)} %trans_hbm.1, bf16[12,128,128]{2,1,0:T(8,128)(2,1)} %tiles_hbm.1, s32[64,64]{1,0:T(8,128)} %pores_hbm.1, bf16[64,512]{1,0:T(8,128)(2,1)} %weight_hbm.1), custom_call_target="tpu_custom_call" | custom-call | tf_op jit(solution)/shard_map/sweep/pallas_call | solution.py:273
  48.1 0.6 %copy.10 = bf16[64,512]{1,0:T(8,128)(2,1)} copy(bf16[64,512]{1,0:T(8,128)(2,1)S(1)} %get-tuple-element.2) | data formatting | bytes 131072
  48.8 0.6 %copy.11 = bf16[12,32,128]{2,1,0:T(8,128)(2,1)} copy(bf16[12,32,128]{2,1,0:T(8,128)(2,1)S(1)} %get-tuple-element.3) | data formatting | bytes 196608

commit v4 on v3

--- a/solution.py
+++ b/solution.py
@@ -34,7 +34,7 @@
 def sweep(
     n_inj, n_blk, blocks, tiles_dev, row_hbm, dest_hbm, trans_hbm, tiles_hbm, pores_hbm, weight_hbm,
     sens_ref, grad_ref, row_in, dest_in, trans_in, tiles, pores, state, adj, adj_t, terms, fsend, bsend, brecv, gsend, grecv,
-    slot_s, tile_s, rowmask, transmask, in_sem, fs_sem, fr_sem, bs_sem, br_sem, gs_sem, gr_sem, *fetched,
+    gsum, slot_s, tile_s, perm_s, place_s, rowmask, transmask, in_sem, fs_sem, fr_sem, bs_sem, br_sem, gs_sem, gr_sem, *fetched,
 ):
     me_i, me_b = lax.axis_index("inj"), lax.axis_index("blk")
     sets = pores.shape[0]
@@ -48,13 +48,20 @@
     def at_inj(distance):
         return lax.rem(me_i + distance, n_inj)
 
+    first = pltpu.make_async_copy(pores_hbm, pores, in_sem.at[0])
+    first.start()
+    barrier = pltpu.get_barrier_semaphore()
+    for j in range(NEIGH, 0, -1):
+        pl.semaphore_signal(barrier, inc=1, device_id=at_blk(offset_of(j)), device_id_type=MESH)
+    for o in range(1, n_inj):
+        pl.semaphore_signal(barrier, inc=1, device_id=(at_inj(o), me_b), device_id_type=MESH)
+
     small = [
         pltpu.make_async_copy(trans_hbm, trans_in, in_sem.at[2 + blocks]),
         pltpu.make_async_copy(row_hbm, row_in, in_sem.at[3 + blocks]),
         pltpu.make_async_copy(dest_hbm, dest_in, in_sem.at[4 + blocks]),
     ]
     loads = [
-        pltpu.make_async_copy(pores_hbm, pores, in_sem.at[0]),
         pltpu.make_async_copy(tiles_hbm, tiles, in_sem.at[1]),
     ]
     for c in range(blocks):
@@ -65,15 +72,8 @@
                 in_sem.at[2 + c],
             )
         )
-    loads[0].start()
-    for load in small + loads[1:]:
+    for load in small + loads:
         load.start()
-
-    barrier = pltpu.get_barrier_semaphore()
-    for j in range(1, NEIGH + 1):
-        pl.semaphore_signal(barrier, inc=1, device_id=at_blk(offset_of(j)), device_id_type=MESH)
-    for o in range(1, n_inj):
-        pl.semaphore_signal(barrier, inc=1, device_id=(at_inj(o), me_b), device_id_type=MESH)
 
     def f_copy(t, h, j, count=1):
         span = pl.ds(j * CAP, count * CAP)
@@ -143,7 +143,7 @@
                 total[c] = kept if total[c] is None else total[c] + kept
         return total
 
-    loads[0].wait()
+    first.wait()
     ids = pores[...]
     low = lax.bitwise_and(ids, width - 1)
     unit = lax.shift_left(jnp.ones_like(ids), lax.shift_right_logical(ids, 7) * 8)
@@ -176,6 +176,17 @@
         for i in range(tiles_dev):
             user = jnp.where(slots[i] == n, i, user)
         tile_s[n] = user
+    before, ranks = jnp.int32(0), []
+    for i in range(tiles_dev):
+        own = dests[i] == 0
+        ranks.append(jnp.where(own, slots[i], CAP + i - before))
+        before = before + jnp.where(own, 1, 0)
+        place_s[i] = ranks[i]
+    for q in range(tiles_dev):
+        user = jnp.int32(0)
+        for i in range(tiles_dev):
+            user = jnp.where(ranks[i] == q, i, user)
+        perm_s[q] = user
     for i in range(tiles_dev):
         for r in range(blocks):
             rowmask[i * blocks + r] = jnp.where(row_in[i] == r, 1.0, 0.0).astype(F32)
@@ -184,12 +195,42 @@
             transmask[n * blocks + c] = jnp.where(trans_in[0, n] == c, 1.0, 0.0).astype(F32)
     terms[tiles_dev] = jnp.zeros_like(terms[tiles_dev])
 
-    for load in loads[1:]:
+    for load in loads:
         load.wait()
     for h in range(HB):
         b_fill(STEPS - 1, h)
     for h in range(HB):
         b_start(STEPS - 1, h)
+
+    def g_copy(part, o):
+        to = at_inj(o)
+        span = pl.ds(CAP, tiles_dev - CAP) if part else pl.ds(0, CAP)
+        return pltpu.make_async_remote_copy(
+            gsend.at[to, span], grecv.at[o - 1, span], gs_sem.at[part, o - 1], gr_sem.at[part, o - 1],
+            device_id=(to, me_b), device_id_type=MESH,
+        )
+
+    def gradient(part):
+        for q in range(CAP, tiles_dev) if part else range(CAP):
+            i = perm_s[q]
+            slot = slot_s[i] if part else q
+            columns = jnp.concatenate([fetched[t * HF + h][slot] for t in range(STEPS) for h in range(HF)], axis=0)
+            full = dot_nn(adj_t[row_in[i]], columns) * (1.0 / sets)
+            full = full.astype(BF16)
+            for p in range(n_inj):
+                gsend[p, q] = full[p * portion : (p + 1) * portion]
+        for o in range(1, n_inj):
+            g_copy(part, o).start()
+
+    def g_sum(part):
+        for o in range(1, n_inj):
+            g_copy(part, o).wait_send()
+            g_copy(part, o).wait_recv()
+        span = pl.ds(CAP, tiles_dev - CAP) if part else pl.ds(0, CAP)
+        mine = gsend[me_i, span].astype(F32)
+        for o in range(1, n_inj):
+            mine = mine + grecv[o - 1, span].astype(F32)
+        gsum[span] = mine.astype(BF16)
 
     def transpose_pair(p):
         for r in range(blocks):
@@ -210,24 +251,7 @@
         if last:
             for h in range(HB):
                 b_start(0, h)
-            for i in range(tiles_dev):
-                columns = jnp.concatenate(
-                    [fetched[t * HF + h][slot_s[i]] for t in range(STEPS) for h in range(HF)], axis=0
-                )
-                full = dot_nn(adj_t[row_in[i]], columns) * (1.0 / sets)
-                full = full.astype(BF16)
-                for p in range(n_inj):
-                    gsend[p, i] = full[p * portion : (p + 1) * portion]
-            g_copies = []
-            for o in range(1, n_inj):
-                to = at_inj(o)
-                g_copies.append(
-                    pltpu.make_async_remote_copy(
-                        gsend.at[to], grecv.at[o - 1], gs_sem.at[o - 1], gr_sem.at[o - 1],
-                        device_id=(to, me_b), device_id_type=MESH,
-                    )
-                )
-                g_copies[-1].start()
+            gradient(1)
         for h in range(HB):
             if k:
                 b_all(back + 1, h).wait_send()
@@ -246,18 +270,15 @@
             transpose_pair(1)
         if k == STEPS - 2:
             transpose_pair(0)
+            gradient(0)
     for h in range(HF):
         f_all(STEPS - 1, h).wait_send()
     for h in range(HB):
         b_all(0, h).wait_send()
-    for copy in g_copies:
-        copy.wait_recv()
-    mine = gsend[me_i].astype(F32)
-    for o in range(1, n_inj):
-        mine = mine + grecv[o - 1].astype(F32)
-    grad_ref[...] = mine.astype(BF16)
-    for copy in g_copies:
-        copy.wait_send()
+    for part in range(2):
+        g_sum(part)
+    for i in range(tiles_dev):
+        grad_ref[i] = gsum[place_s[i]]
 
 
 def shards(tile_values, tile_row, tile_dest, trans_block, inj_pores, final_weight):
@@ -291,8 +312,11 @@
             pltpu.VMEM((STEPS, HB, SLOTS, bs, width), BF16),
             pltpu.VMEM((n_inj, tiles_dev, portion, width), BF16),
             pltpu.VMEM((n_inj - 1, tiles_dev, portion, width), BF16),
+            pltpu.VMEM((tiles_dev, portion, width), BF16),
             pltpu.SMEM((tiles_dev,), jnp.int32),
             pltpu.SMEM((SLOTS,), jnp.int32),
+            pltpu.SMEM((tiles_dev,), jnp.int32),
+            pltpu.SMEM((tiles_dev,), jnp.int32),
             pltpu.SMEM((tiles_dev * blocks,), F32),
             pltpu.SMEM((SLOTS * blocks,), F32),
             dma((5 + blocks,)),
@@ -300,8 +324,8 @@
             dma((STEPS, HF)),
             dma((STEPS, HB)),
             dma((STEPS, HB)),
-            dma((n_inj - 1,)),
-            dma((n_inj - 1,)),
+            dma((2, n_inj - 1)),
+            dma((2, n_inj - 1)),
         ]
         + [pltpu.VMEM((SLOTS, fs, width), BF16)] * (STEPS * HF),
         compiler_params=pltpu.CompilerParams(

time: 49.5 us -> 48.4 us (0.978)
  Pallas kernels: 47.5 us -> 46.4 us
    pallas_call x1, Pallas kernels: 47.5 us -> 46.4 us  [shards(): pl.pallas_call(functools.partial(sweep, n_inj, n_blk, blocks, tiles_dev),...]
where the time goes in v4:
time: 48.4 us; the launch traced here: 48.3 us
  Pallas kernels  46.4 us (96%)
  local copies, waits for them, and re-layouts  1.27 us (3%)
  between operations  0.64 us (1%)
    pallas_call x1, Pallas kernels, shards(): pl.pallas_call(functools.partial(sweep, n_inj, n_blk, blocks, tiles_dev),...  46.4 us
    unnamed x2, local copies, waits for them, and re-layouts  1.27 us

profile of v4, /device:TPU:1, one launch (start us, length us, event | category | flops | bytes accessed | tf_op | source)
XLA Modules:
  0.0 48.3 jit_solution(4014374898905281220)
XLA Ops:
  0.6 46.4 %sweep.1 = (bf16[64,512]{1,0:T(8,128)(2,1)S(1)}, bf16[12,32,128]{2,1,0:T(8,128)(2,1)S(1)}) custom-call(s32[12]{0:T(128)} %row_hbm.1, s32[12]{0:T(128)} %bitcast.1, s32[1,21]{1,0:T(1,128)} %trans_hbm.1, bf16[12,128,128]{2,1,0:T(8,128)(2,1)} %tiles_hbm.1, s32[64,64]{1,0:T(8,128)} %pores_hbm.1, bf16[64,512]{1,0:T(8,128)(2,1)} %weight_hbm.1), custom_call_target="tpu_custom_call" | custom-call | tf_op jit(solution)/shard_map/sweep/pallas_call | solution.py:294
  47.0 0.6 %copy.10 = bf16[64,512]{1,0:T(8,128)(2,1)} copy(bf16[64,512]{1,0:T(8,128)(2,1)S(1)} %get-tuple-element.2) | data formatting | bytes 131072
  47.7 0.6 %copy.11 = bf16[12,32,128]{2,1,0:T(8,128)(2,1)} copy(bf16[12,32,128]{2,1,0:T(8,128)(2,1)S(1)} %get-tuple-element.3) | data formatting | bytes 196608

commit v5 on v4

--- a/solution.py
+++ b/solution.py
@@ -11,6 +11,7 @@
 STEPS = 4
 CAP = 3
 SLOTS = (NEIGH + 1) * CAP
+ORDER = (3, 4, 5, 6, 1, 2)
 HF = 2
 HB = 2
 MESH = pl.DeviceIdType.MESH
@@ -92,14 +93,14 @@
         )
 
     def f_start(t, h):
-        for j in range(1, NEIGH + 1):
+        for j in ORDER:
             f_copy(t, h, j).start()
 
     def f_all(t, h):
         return f_copy(t, h, 1, NEIGH)
 
     def b_start(t, h):
-        for j in range(1, NEIGH + 1):
+        for j in ORDER:
             b_copy(t, h, j).start()
 
     def b_all(t, h):
@@ -219,7 +220,7 @@
             full = full.astype(BF16)
             for p in range(n_inj):
                 gsend[p, q] = full[p * portion : (p + 1) * portion]
-        for o in range(1, n_inj):
+        for o in sorted(range(1, n_inj), key=lambda o: -min(o, n_inj - o)):
             g_copy(part, o).start()
 
     def g_sum(part):
@@ -237,40 +238,47 @@
             both = adj[r, pl.ds(p * 2 * sets, 2 * sets)]
             adj_t[r, :, pl.ds(p * 2 * sets, 2 * sets)] = both.T
 
-    for k in range(STEPS):
-        last = k == STEPS - 1
-        back = STEPS - 1 - k
+    def f_turn(k, h):
+        if k:
+            f_all(k - 1, h).wait_send()
+        f_all(k, h).wait_recv()
+        if k < STEPS - 1:
+            f_step(k, h)
+            f_fill(k + 1, h)
+            f_start(k + 1, h)
+
+    def b_turn(back, h):
+        if back < STEPS - 1:
+            b_all(back + 1, h).wait_send()
+        b_all(back, h).wait_recv()
+        total = b_step(back, h)
+        for c in range(blocks):
+            if back:
+                adj[c, pl.ds((back - 1) * sets + h * bs, bs)] = total[c].astype(BF16)
+            else:
+                sens_ref[pl.ds(h * bs, bs), pl.ds(c * width, width)] = total[c].astype(BF16)
+        if back:
+            b_fill(back - 1, h)
+            if back > 1:
+                b_start(back - 1, h)
+
+    for k in range(STEPS - 1):
         for h in range(HF):
-            if k:
-                f_all(k - 1, h).wait_send()
-            f_all(k, h).wait_recv()
-            if not last:
-                f_step(k, h)
-                f_fill(k + 1, h)
-                f_start(k + 1, h)
-        if last:
-            for h in range(HB):
-                b_start(0, h)
-            gradient(1)
+            f_turn(k, h)
         for h in range(HB):
-            if k:
-                b_all(back + 1, h).wait_send()
-            b_all(back, h).wait_recv()
-            total = b_step(back, h)
-            for c in range(blocks):
-                if last:
-                    sens_ref[pl.ds(h * bs, bs), pl.ds(c * width, width)] = total[c].astype(BF16)
-                else:
-                    adj[c, pl.ds((back - 1) * sets + h * bs, bs)] = total[c].astype(BF16)
-            if not last:
-                b_fill(back - 1, h)
-                if back > 1:
-                    b_start(back - 1, h)
+            b_turn(STEPS - 1 - k, h)
         if k == 0:
             transpose_pair(1)
         if k == STEPS - 2:
             transpose_pair(0)
             gradient(0)
+    for h in range(HF):
+        f_turn(STEPS - 1, h)
+    for h in range(HB):
+        b_start(0, h)
+    gradient(1)
+    for h in range(HB):
+        b_turn(0, h)
     for h in range(HF):
         f_all(STEPS - 1, h).wait_send()
     for h in range(HB):

time: 48.4 us -> 48.3 us (level)
  no operation moved by 1% of the time
where the time goes in v5:
time: 48.3 us; the launch traced here: 48.2 us
  Pallas kernels  46.3 us (96%)
  local copies, waits for them, and re-layouts  1.27 us (3%)
  between operations  0.64 us (1%)
    pallas_call x1, Pallas kernels, shards(): pl.pallas_call(functools.partial(sweep, n_inj, n_blk, blocks, tiles_dev),...  46.3 us
    unnamed x2, local copies, waits for them, and re-layouts  1.27 us

profile of v5, /device:TPU:1, one launch (start us, length us, event | category | flops | bytes accessed | tf_op | source)
XLA Modules:
  0.0 48.2 jit_solution(16293752241390291746)
XLA Ops:
  0.6 46.3 %sweep.1 = (bf16[64,512]{1,0:T(8,128)(2,1)S(1)}, bf16[12,32,128]{2,1,0:T(8,128)(2,1)S(1)}) custom-call(s32[12]{0:T(128)} %row_hbm.1, s32[12]{0:T(128)} %bitcast.1, s32[1,21]{1,0:T(1,128)} %trans_hbm.1, bf16[12,128,128]{2,1,0:T(8,128)(2,1)} %tiles_hbm.1, s32[64,64]{1,0:T(8,128)} %pores_hbm.1, bf16[64,512]{1,0:T(8,128)(2,1)} %weight_hbm.1), custom_call_target="tpu_custom_call" | custom-call | tf_op jit(solution)/shard_map/sweep/pallas_call | solution.py:302
  46.9 0.6 %copy.10 = bf16[64,512]{1,0:T(8,128)(2,1)} copy(bf16[64,512]{1,0:T(8,128)(2,1)S(1)} %get-tuple-element.2) | data formatting | bytes 131072
  47.6 0.6 %copy.11 = bf16[12,32,128]{2,1,0:T(8,128)(2,1)} copy(bf16[12,32,128]{2,1,0:T(8,128)(2,1)S(1)} %get-tuple-element.3) | data formatting | bytes 196608

commit v6 on v5

--- a/solution.py
+++ b/solution.py
@@ -203,16 +203,18 @@
     for h in range(HB):
         b_start(STEPS - 1, h)
 
+    cuts = (0, CAP, (CAP + tiles_dev + 1) // 2, tiles_dev)
+
     def g_copy(part, o):
         to = at_inj(o)
-        span = pl.ds(CAP, tiles_dev - CAP) if part else pl.ds(0, CAP)
+        span = pl.ds(cuts[part], cuts[part + 1] - cuts[part])
         return pltpu.make_async_remote_copy(
             gsend.at[to, span], grecv.at[o - 1, span], gs_sem.at[part, o - 1], gr_sem.at[part, o - 1],
             device_id=(to, me_b), device_id_type=MESH,
         )
 
     def gradient(part):
-        for q in range(CAP, tiles_dev) if part else range(CAP):
+        for q in range(cuts[part], cuts[part + 1]):
             i = perm_s[q]
             slot = slot_s[i] if part else q
             columns = jnp.concatenate([fetched[t * HF + h][slot] for t in range(STEPS) for h in range(HF)], axis=0)
@@ -227,7 +229,7 @@
         for o in range(1, n_inj):
             g_copy(part, o).wait_send()
             g_copy(part, o).wait_recv()
-        span = pl.ds(CAP, tiles_dev - CAP) if part else pl.ds(0, CAP)
+        span = pl.ds(cuts[part], cuts[part + 1] - cuts[part])
         mine = gsend[me_i, span].astype(F32)
         for o in range(1, n_inj):
             mine = mine + grecv[o - 1, span].astype(F32)
@@ -277,14 +279,16 @@
     for h in range(HB):
         b_start(0, h)
     gradient(1)
+    gradient(2)
+    g_sum(0)
     for h in range(HB):
         b_turn(0, h)
     for h in range(HF):
         f_all(STEPS - 1, h).wait_send()
     for h in range(HB):
         b_all(0, h).wait_send()
-    for part in range(2):
-        g_sum(part)
+    g_sum(1)
+    g_sum(2)
     for i in range(tiles_dev):
         grad_ref[i] = gsum[place_s[i]]
 
@@ -332,8 +336,8 @@
             dma((STEPS, HF)),
             dma((STEPS, HB)),
             dma((STEPS, HB)),
-            dma((2, n_inj - 1)),
-            dma((2, n_inj - 1)),
+            dma((3, n_inj - 1)),
+            dma((3, n_inj - 1)),
         ]
         + [pltpu.VMEM((SLOTS, fs, width), BF16)] * (STEPS * HF),
         compiler_params=pltpu.CompilerParams(

time: 48.3 us -> 47.8 us (0.990)
  Pallas kernels: 46.3 us -> 45.8 us
    pallas_call x1, Pallas kernels: 46.3 us -> 45.8 us  [shards(): pl.pallas_call(functools.partial(sweep, n_inj, n_blk, blocks, tiles_dev),...]
where the time goes in v6:
time: 47.8 us; the launch traced here: 47.7 us
  Pallas kernels  45.8 us (96%)
  local copies, waits for them, and re-layouts  1.27 us (3%)
  between operations  0.64 us (1%)
    pallas_call x1, Pallas kernels, shards(): pl.pallas_call(functools.partial(sweep, n_inj, n_blk, blocks, tiles_dev),...  45.8 us
    unnamed x2, local copies, waits for them, and re-layouts  1.27 us

profile of v6, /device:TPU:1, one launch (start us, length us, event | category | flops | bytes accessed | tf_op | source)
XLA Modules:
  0.0 47.7 jit_solution(13256005844767670741)
XLA Ops:
  0.6 45.8 %sweep.1 = (bf16[64,512]{1,0:T(8,128)(2,1)S(1)}, bf16[12,32,128]{2,1,0:T(8,128)(2,1)S(1)}) custom-call(s32[12]{0:T(128)} %row_hbm.1, s32[12]{0:T(128)} %bitcast.1, s32[1,21]{1,0:T(1,128)} %trans_hbm.1, bf16[12,128,128]{2,1,0:T(8,128)(2,1)} %tiles_hbm.1, s32[64,64]{1,0:T(8,128)} %pores_hbm.1, bf16[64,512]{1,0:T(8,128)(2,1)} %weight_hbm.1), custom_call_target="tpu_custom_call" | custom-call | tf_op jit(solution)/shard_map/sweep/pallas_call | solution.py:306
  46.4 0.6 %copy.10 = bf16[64,512]{1,0:T(8,128)(2,1)} copy(bf16[64,512]{1,0:T(8,128)(2,1)S(1)} %get-tuple-element.2) | data formatting | bytes 131072
  47.0 0.6 %copy.11 = bf16[12,32,128]{2,1,0:T(8,128)(2,1)} copy(bf16[12,32,128]{2,1,0:T(8,128)(2,1)S(1)} %get-tuple-element.3) | data formatting | bytes 196608

commit v7 on v6

--- a/solution.py
+++ b/solution.py
@@ -11,7 +11,7 @@
 STEPS = 4
 CAP = 3
 SLOTS = (NEIGH + 1) * CAP
-ORDER = (3, 4, 5, 6, 1, 2)
+ORDER = (1, 2, 3, 4, 5, 6)
 HF = 2
 HB = 2
 MESH = pl.DeviceIdType.MESH

time: 47.8 us -> 48.2 us (level)
  no operation moved by 1% of the time
where the time goes in v7:
time: 48.2 us; the launch traced here: 48.1 us
  Pallas kernels  46.1 us (96%)
  local copies, waits for them, and re-layouts  1.27 us (3%)
  between operations  0.64 us (1%)
    pallas_call x1, Pallas kernels, shards(): pl.pallas_call(functools.partial(sweep, n_inj, n_blk, blocks, tiles_dev),...  46.1 us
    unnamed x2, local copies, waits for them, and re-layouts  1.27 us

profile of v7, /device:TPU:1, one launch (start us, length us, event | category | flops | bytes accessed | tf_op | source)
XLA Modules:
  0.0 48.1 jit_solution(7633279867947570771)
XLA Ops:
  0.6 46.1 %sweep.1 = (bf16[64,512]{1,0:T(8,128)(2,1)S(1)}, bf16[12,32,128]{2,1,0:T(8,128)(2,1)S(1)}) custom-call(s32[12]{0:T(128)} %row_hbm.1, s32[12]{0:T(128)} %bitcast.1, s32[1,21]{1,0:T(1,128)} %trans_hbm.1, bf16[12,128,128]{2,1,0:T(8,128)(2,1)} %tiles_hbm.1, s32[64,64]{1,0:T(8,128)} %pores_hbm.1, bf16[64,512]{1,0:T(8,128)(2,1)} %weight_hbm.1), custom_call_target="tpu_custom_call" | custom-call | tf_op jit(solution)/shard_map/sweep/pallas_call | solution.py:306
  46.8 0.6 %copy.10 = bf16[64,512]{1,0:T(8,128)(2,1)} copy(bf16[64,512]{1,0:T(8,128)(2,1)S(1)} %get-tuple-element.2) | data formatting | bytes 131072
  47.4 0.6 %copy.11 = bf16[12,32,128]{2,1,0:T(8,128)(2,1)} copy(bf16[12,32,128]{2,1,0:T(8,128)(2,1)S(1)} %get-tuple-element.3) | data formatting | bytes 196608
